TPU v7x, 256 devices: a whole 4x4x8 slice. The times are simulated.
256 devices in a mesh: tm: 128 (over y, z, x), space: 2 (over core).
Axes of the slice: x: 4, y: 4, z: 8, core: 2. Of those that a mesh axis runs over, the one named last changes fastest.
Arguments:
- cpoints: float32 [1024, 32, 512], P('tm', 'space'), may hold values from -7 to 7
- initial: float32 [32, 512], P('space'), may hold values from -6 to 6
- diffusion: float32 [32, 512], P('space'), may hold values from 0.0005 to 0.0025
- velocity_x: float32 [32, 512], P('space'), may hold values from -0.0025 to 0.0025
- velocity_y: float32 [32, 512], P('space'), may hold values from -0.0025 to 0.0025
- source: float32 [32, 512], P('space'), may hold values from -0.018 to 0.018
Outputs:
- updated: float32 [1024, 32, 512], P('tm', 'space')
All inputs are finite; a program needn't handle non-finite values.
Results may differ from a plain program's by a relative error of at most 0.000032.
Values sent between devices are 32-bit elements; how exact they have to be, the bound alone decides.
A program may use at most 64 MiB of HBM per device.

v0:
```python
import jax
import jax.numpy as jnp
from jax import lax
from jax.sharding import PartitionSpec as P

M = 8


def with_halo(array, sides, width):
    for axis, dim in sides:
        peers, length = (lax.axis_size(axis), array.shape[dim])
        up = [(i, (i + 1) % peers) for i in range(peers - 1)]
        down = [(j, i) for i, j in up]
        last = lax.slice_in_dim(array, length - width, length, axis=dim)
        initial = lax.slice_in_dim(array, 0, width, axis=dim)
        before = lax.ppermute(last, axis, up)
        after = lax.ppermute(initial, axis, down)
        array = jnp.concatenate([before, array, after], axis=dim)
    return array


def shifted(value, axis, steps):
    count = lax.axis_size(axis)
    initial, last = (max(0, -steps), min(count, count - steps))
    return lax.ppermute(value, axis, [(source, source + steps) for source in range(initial, last)])


def stencil(padded, diffusion, velocity_x, velocity_y, time_scale):
    centre = padded[..., 1:-1, :]
    upper_row = padded[..., :-2, :]
    lower_row = padded[..., 2:, :]
    right_col = jnp.roll(centre, -1, axis=-1)
    left_col = jnp.roll(centre, 1, axis=-1)
    spread = upper_row + lower_row + right_col + left_col - 4.0 * centre
    across = jnp.maximum(velocity_x, 0.0) * (centre - left_col) + jnp.minimum(velocity_x, 0.0) * (
        right_col - centre
    )
    downward = jnp.maximum(velocity_y, 0.0) * (centre - upper_row) + jnp.minimum(
        velocity_y, 0.0
    ) * (lower_row - centre)
    return centre + time_scale * (diffusion * spread - across - downward)


def band_step(states, coeffs, time_scale):
    padded = with_halo(states, (("space", 1),), 1)
    return stencil(padded, coeffs[0], coeffs[1], coeffs[2], time_scale)


def grid_step(states, coeffs, time_scale):
    padded = jnp.pad(states, ((0, 0), (1, 1), (0, 0)))
    return stencil(padded, coeffs[0], coeffs[1], coeffs[2], time_scale)


def previous(last_state, opening):
    arrived = shifted(last_state, "tm", 1)
    return jnp.where(lax.axis_index("tm") == 0, opening, arrived)


def body(cpoints, initial, diffusion, velocity_x, velocity_y, source):
    coeffs = jnp.stack([diffusion, velocity_x, velocity_y])
    band_rows = cpoints.shape[1]
    columns = cpoints.shape[2]
    slab_idx = lax.axis_index("tm")
    band_idx = lax.axis_index("space")
    n_slabs = lax.axis_size("tm")
    zeros_state = jnp.zeros((1, band_rows, columns), jnp.float32)
    opening = initial[None]

    def relax_fine(states):
        for _ in range(M):
            states = band_step(states, coeffs, 1.0) + source
        return states

    def level_move(states, time_scale):
        return band_step(states, coeffs, time_scale)

    relaxed = relax_fine(jnp.concatenate([previous(cpoints[-1:], opening), cpoints[:-1]], axis=0))
    defect = (
        relax_fine(jnp.concatenate([previous(relaxed[-1:], opening), relaxed[:-1]], axis=0))
        - relaxed
    )
    level_c = zeros_state
    for counter in range(M):
        level_c = level_move(level_c, 8.0) + defect[counter : counter + 1]
    lagged = previous(level_c, zeros_state)
    states = lagged
    for _ in range(M):
        states = band_step(states, coeffs, 8.0)
    whole_coef = lax.all_gather(coeffs, "space", axis=1, tiled=True)
    rows_all = lax.all_gather(states, "space", axis=1, tiled=True)
    gathered = lax.all_gather(rows_all, "tm", axis=0, tiled=True)
    start_grid = jnp.zeros((1, gathered.shape[1], columns), jnp.float32)

    def coarse_step(step_idx, carried):
        current, retained = carried
        addend = lax.dynamic_index_in_dim(gathered, step_idx, 0, True)
        current = grid_step(current, whole_coef, 64.0) + addend
        retained = jnp.where(step_idx == slab_idx - 1, current, retained)
        return (current, retained)

    _, before = lax.fori_loop(0, n_slabs - 1, coarse_step, (start_grid, start_grid))
    earlier = lax.dynamic_slice_in_dim(before, band_idx * band_rows, band_rows, 1)
    current = level_move(earlier, 64.0) + states
    corrected = level_c + current
    walker = lagged + earlier
    errors = []
    for counter in range(M - 1):
        walker = level_move(walker, 8.0) + defect[counter : counter + 1]
        errors.append(walker)
    errors.append(corrected)
    return relaxed + jnp.concatenate(errors, axis=0)


def solution(mesh):
    placed = (
        P("tm", "space", None),
        P("space", None),
        P("space", None),
        P("space", None),
        P("space", None),
        P("space", None),
    )
    return jax.shard_map(
        body, mesh=mesh, in_specs=placed, out_specs=P("tm", "space", None), check_vma=False
    )
```

profile of v0, /device:TPU:25, one launch (start us, length us, event | category | flops | bytes accessed | tf_op | source)
XLA Modules:
  0.0 531.1 jit_solution(250952655946509666)
XLA Ops:
  7.3 3.1 collective-permute-start
  12.2 6.3 %collective-permute-done = f32[1,16,512]{2,1,0:T(8,128)S(1)} collective-permute-done((f32[1,16,512]{2,1,0:T(8,128)S(1)}, f32[1,16,512]{2,1,0:T(8,128)S(1)}, u32[]{:S(2)}, u32[]{:S(2)}) %collective-permute-start) | collective-permute-done | bytes 32800 | tf_op jit(solution)/shard_map/ppermute | solution.py:25
  20.7 3.4 collective-permute-start.2
  27.5 3.0 collective-permute-start.4
  33.9 3.0 collective-permute-start.6
  40.3 3.0 collective-permute-start.8
  51.7 3.0 collective-permute-start.12
  57.3 3.0 collective-permute-start.14
  62.9 3.0 collective-permute-start.16
  77.4 3.4 collective-permute-start.21
  83.4 3.0 collective-permute-start.23
  89.0 3.0 collective-permute-start.25
  94.6 3.0 collective-permute-start.27
  100.2 3.0 collective-permute-start.29
  105.8 3.0 collective-permute-start.31
  111.5 3.0 collective-permute-start.33
  117.1 3.0 collective-permute-start.35
  122.7 3.0 collective-permute-start.37
  165.7 6.9 %collective-permute-done.50 = f32[1,16,512]{2,1,0:T(8,128)S(1)} collective-permute-done((f32[1,16,512]{2,1,0:T(8,128)S(1)}, f32[1,16,512]{2,1,0:T(8,128)S(1)}, u32[]{:S(2)}, u32[]{:S(2)}) %collective-permute-start.50) | collective-permute-done | bytes 32800 | tf_op jit(solution)/shard_map/ppermute | solution.py:25
  174.1 3.4 collective-permute-start.52
  185.0 3.2 collective-permute-start.56
  219.5 114.5 %all-gather.2.cloned.1.call-done = f32[128,32,512]{2,1,0:T(8,128)} async-done(((f32[1,32,512]{2,1,0:T(8,128)}), f32[128,32,512]{2,1,0:T(8,128)}) %all-gather.2.cloned.1.call-update) | async-done | bytes 8388624 | tf_op jit(solution)/shard_map/all_gather | solution.py:91
  334.0 146.2 %while.18 = (s32[]{:T(128)}, f32[1,32,512]{2,1,0:T(8,128)S(1)}, f32[1,32,512]{2,1,0:T(8,128)S(1)}, f32[3,32,512]{2,1,0:T(8,128)S(1)}, f32[128,32,512]{2,1,0:T(8,128)}, /*index=5*/s32[]{:T(128)}, s32[]{:T(128)}, s32[]{:T(128)}) while((s32[]{:T(128)}, f32[1,32,512]{2,1,0:T(8,128)S(1)}, f32[1,32,512]{2,1,0:T(8,128)S(1)}, ...), condition=%wide.region_1.2_spmd.clone, body=%wide.region_0.1_spmd.clone.sunk | while | flops 491524 | bytes 1048686 | solution.py:101
  481.7 5.3 collective-permute-start.68
  (843 shorter events, 320.7 us)
Async XLA Ops:
  6.5 327.4 %all-gather.2.cloned.1.call-start = ((), (), s32[]{:S(2)}) async-start(), calls=%async_computation | async-start | bytes 8454144 | tf_op jit(solution)/shard_map/all_gather | solution.py:91
  7.3 11.1 %collective-permute-start = (f32[1,16,512]{2,1,0:T(8,128)S(1)}, f32[1,16,512]{2,1,0:T(8,128)S(1)}, u32[]{:S(2)}, u32[]{:S(2)}) collective-permute-start(f32[1,16,512]{2,1,0:T(8,128)S(1)} %slice.1176), channel_id=1, source_target_pairs={{0,2},{2,4},{4,6},{6,8},{8,10},{10,12},{12,14},{14,16},{16,18},{18... | collective-permute-start | bytes 98312 | tf_op jit(solution)/shard_map/ppermute | solution.py:25
  19.4 4.8 collective-permute-start.1
  26.2 4.4 collective-permute-start.3
  32.6 4.4 collective-permute-start.5
  39.0 4.4 collective-permute-start.7
  50.4 4.4 collective-permute-start.11
  56.0 4.4 collective-permute-start.13
  61.6 4.4 collective-permute-start.15
  67.0 8.9 %collective-permute-start.19 = (f32[1,16,512]{2,1,0:T(8,128)S(1)}, f32[1,16,512]{2,1,0:T(8,128)S(1)}, u32[]{:S(2)}, u32[]{:S(2)}) collective-permute-start(f32[1,16,512]{2,1,0:T(8,128)S(1)} %slice.1570), channel_id=1, source_target_pairs={{0,2},{2,4},{4,6},{6,8},{8,10},{10,12},{12,14},{14,16},{16,18},{18... | collective-permute-start | bytes 98312 | tf_op jit(solution)/shard_map/ppermute | solution.py:25
  69.0 52.3 %collective-permute-start.17 = (f32[1,1,512]{2,1,0:T(1,128)S(1)}, f32[1,1,512]{2,1,0:T(1,128)S(1)}, u32[]{:S(2)}, u32[]{:S(2)}) collective-permute-start(f32[1,1,512]{2,1,0:T(1,128)S(1)} %broadcast.88), channel_id=1, source_target_pairs={{0,1},{2,3},{4,5},{6,7},{8,9},{10,11},{12,13},{14,15},{16,17},{18,... | collective-permute-start | bytes 6152 | tf_op jit(solution)/shard_map/ppermute | solution.py:16
  70.3 51.0 %collective-permute-start.18 = (f32[1,1,512]{2,1,0:T(1,128)S(1)}, f32[1,1,512]{2,1,0:T(1,128)S(1)}, u32[]{:S(2)}, u32[]{:S(2)}) collective-permute-start(f32[1,1,512]{2,1,0:T(1,128)S(1)} %broadcast.88), channel_id=1, source_target_pairs={{1,0},{3,2},{5,4},{7,6},{9,8},{11,10},{13,12},{15,14},{17,16},{19,... | collective-permute-start | bytes 6152 | tf_op jit(solution)/shard_map/ppermute | solution.py:17
  76.1 4.8 collective-permute-start.20
  82.1 4.4 collective-permute-start.22
  87.7 4.4 collective-permute-start.24
  93.3 4.4 collective-permute-start.26
  98.9 4.4 collective-permute-start.28
  163.8 8.9 %collective-permute-start.50 = (f32[1,16,512]{2,1,0:T(8,128)S(1)}, f32[1,16,512]{2,1,0:T(8,128)S(1)}, u32[]{:S(2)}, u32[]{:S(2)}) collective-permute-start(f32[1,16,512]{2,1,0:T(8,128)S(1)} %slice_add_fusion), channel_id=1, source_target_pairs={{0,2},{2,4},{4,6},{6,8},{8,10},{10,12},{12,14},{14,16},{16,18},{18... | collective-permute-start | bytes 98312 | tf_op jit(solution)/shard_map/ppermute | solution.py:25
  172.8 4.8 collective-permute-start.51
  183.7 4.6 collective-permute-start.55
  480.4 11.1 %collective-permute-start.67 = (f32[1,1,512]{2,1,0:T(1,128)S(1)}, f32[1,1,512]{2,1,0:T(1,128)S(1)}, u32[]{:S(2)}, u32[]{:S(2)}) collective-permute-start(f32[1,1,512]{2,1,0:T(1,128)S(1)} %get-tuple-element.354), channel_id=1, source_target_pairs={{0,1},{2,3},{4,5},{6,7},{8,9},{10,11},{12,13},{14,15},{16,17},{18,... | collective-permute-start | bytes 6152 | tf_op jit(solution)/shard_map/ppermute | solution.py:16
  481.7 9.8 %collective-permute-start.68 = (f32[1,1,512]{2,1,0:T(1,128)S(1)}, f32[1,1,512]{2,1,0:T(1,128)S(1)}, u32[]{:S(2)}, u32[]{:S(2)}) collective-permute-start(f32[1,1,512]{2,1,0:T(1,128)S(1)} %get-tuple-element.355), channel_id=1, source_target_pairs={{1,0},{3,2},{5,4},{7,6},{9,8},{11,10},{13,12},{15,14},{17,16},{19,... | collective-permute-start | bytes 6152 | tf_op jit(solution)/shard_map/ppermute | solution.py:17
  487.0 36.4 %collective-permute-start.81 = (f32[1,1,512]{2,1,0:T(1,128)S(1)}, f32[1,1,512]{2,1,0:T(1,128)S(1)}, u32[]{:S(2)}, u32[]{:S(2)}) collective-permute-start(f32[1,1,512]{2,1,0:T(1,128)S(1)} %get-tuple-element.316), channel_id=1, source_target_pairs={{0,1},{2,3},{4,5},{6,7},{8,9},{10,11},{12,13},{14,15},{16,17},{18,... | collective-permute-start | bytes 6152 | tf_op jit(solution)/shard_map/ppermute | solution.py:16
  488.3 35.1 %collective-permute-start.82 = (f32[1,1,512]{2,1,0:T(1,128)S(1)}, f32[1,1,512]{2,1,0:T(1,128)S(1)}, u32[]{:S(2)}, u32[]{:S(2)}) collective-permute-start(f32[1,1,512]{2,1,0:T(1,128)S(1)} %get-tuple-element.317), channel_id=1, source_target_pairs={{1,0},{3,2},{5,4},{7,6},{9,8},{11,10},{13,12},{15,14},{17,16},{19,... | collective-permute-start | bytes 6152 | tf_op jit(solution)/shard_map/ppermute | solution.py:17
  (67 other events, 798.7 us)
Sparse Core Ops, SparseCore 0:
  217.6 116.2 all-gather.1
where the time goes:
time: 541 us; the launch traced here: 531 us
  starting transfers between devices  182 us (34%)
  waiting for transfers between devices  158 us (29%)
  other arithmetic  140 us (26%)
  local copies, waits for them, and re-layouts  27.9 us (5%)
  between operations  14.7 us (3%)
    ppermute x40, starting transfers between devices, with_halo(): after = lax.ppermute(initial, axis, down)  124 us
    select_n x127, other arithmetic, coarse_step(): retained = jnp.where(step_idx == slab_idx - 1, current, retained)  122 us
    all_gather x1, waiting for transfers between devices, body(): gathered = lax.all_gather(rows_all, 'tm', axis=0, tiled=True)  114 us
    ppermute x40, starting transfers between devices, with_halo(): before = lax.ppermute(last, axis, up)  51.6 us
    ppermute x40, waiting for transfers between devices, with_halo(): after = lax.ppermute(initial, axis, down)  26.1 us
    slice x267, local copies, waits for them, and re-layouts, stencil(): right_col = jnp.roll(centre, -1, axis=-1)  20.1 us
    ppermute x3, waiting for transfers between devices, shifted(): lax.ppermute(value, axis, [(source, source + steps) for source in range(i...  15.8 us
  transfers between devices with their start and end apart: 84, of which 41 were waited for; matrix products, arithmetic and copies ran while one was open for 2% of the time, Pallas kernels for 0%

commit v1 on v0

v1 whole, which is shorter than its diff:
```python
import functools

import jax
import jax.numpy as jnp
from jax import lax
from jax.experimental import pallas as pl
from jax.experimental.pallas import tpu as pltpu
from jax.sharding import PartitionSpec as P

M = 8
NX = 4
NZ = 8
C = 4
R = 4
T = (8, 128)
STATE = (C, R) + T
WIN = (R,) + T
MESH = pl.DeviceIdType.MESH
COLS = [pl.ds(128 * c, 128) for c in range(C)]


def load_state(ref, *idx):
    return [[ref[(*idx, c, r)] for r in range(R)] for c in range(C)]


def store_state(ref, v, *idx):
    for c in range(C):
        for r in range(R):
            ref[(*idx, c, r)] = v[c][r]


def load_win(ref, *idx):
    return [ref[(*idx, r)] for r in range(R)]


def store_win(ref, v, *idx):
    for r in range(R):
        ref[(*idx, r)] = v[r]


def add(a, b):
    if isinstance(a, list):
        return [add(x, y) for x, y in zip(a, b)]
    return a + b


def sub(a, b):
    if isinstance(a, list):
        return [sub(x, y) for x, y in zip(a, b)]
    return a - b


def lanes():
    return lax.broadcasted_iota(jnp.int32, T, 1)


def sublanes():
    return lax.broadcasted_iota(jnp.int32, T, 0)


def ups(column):
    return [pltpu.roll(column[R - 1], 1, 0)] + column[: R - 1]


def downs(column):
    return column[1:] + [pltpu.roll(column[0], 7, 0)]


def full_step(states, coef, source=None):
    lane = lanes()
    first, last = lane == 0, lane == 127
    out = [[[None] * R for _ in range(C)] for _ in states]
    rolled = []
    for v in states:
        to_right = [[pltpu.roll(v[c][r], 1, 1) for r in range(R)] for c in range(C)]
        to_left = [[pltpu.roll(v[c][r], 127, 1) for r in range(R)] for c in range(C)]
        rolled.append((to_right, to_left))
    for c in range(C):
        above = [ups(v[c]) for v in states]
        below = [downs(v[c]) for v in states]
        for r in range(R):
            k0, kl, kr, ku, kd = (coef[k, c, r] for k in range(5))
            plus = None if source is None else source[c, r]
            for n, v in enumerate(states):
                to_right, to_left = rolled[n]
                left = jnp.where(first, to_right[(c - 1) % C][r], to_right[c][r])
                right = jnp.where(last, to_left[(c + 1) % C][r], to_left[c][r])
                new = (k0 * v[c][r] + kl * left) + (kr * right + ku * above[n][r])
                new = new + kd * below[n][r]
                out[n][c][r] = new if plus is None else new + plus
    return out


def win_step(v, coef):
    above, below = ups(v), downs(v)
    out = []
    for r in range(R):
        left, right = pltpu.roll(v[r], 1, 1), pltpu.roll(v[r], 127, 1)
        k0, kl, kr, ku, kd = (coef[k, r] for k in range(5))
        out.append((k0 * v[r] + kl * left) + (kr * right + ku * above[r]) + kd * below[r])
    return out


def full_steps(count, states, coef, source=None):
    return lax.fori_loop(0, count, lambda _, s: full_step(s, coef, source), states)


def win_steps(count, v, coef):
    return lax.fori_loop(0, count, lambda _, s: win_step(s, coef), v)


def window_tiles(v, band):
    lane = lanes()
    low = band == 0
    shift = jnp.where(low, 32, 96)
    take = jnp.logical_or(
        jnp.logical_and(low, lane < 32), jnp.logical_and(jnp.logical_not(low), lane >= 96)
    )
    rot = [[pltpu.roll(v[c][r], shift, 1) for r in range(R)] for c in range(C)]
    out = []
    for c in range(C):
        tile = []
        for r in range(R):
            beside = jnp.where(low, rot[(c - 1) % C][r], rot[(c + 1) % C][r])
            tile.append(jnp.where(take, beside, rot[c][r]))
        out.append(tile)
    return out


def merged(own, other, band):
    lane = lanes()
    low = band == 0
    out = []
    for a, b in zip(own, other):
        w0, w1 = jnp.where(low, a, b), jnp.where(low, b, a)
        out.append(jnp.where(lane < 64, pltpu.roll(w0, 96, 1), pltpu.roll(w1, 32, 1)))
    return out


def kernel(
    n_tm, cpoints, initial, diffusion, velocity_x, velocity_y, source, out,
    cp, fld, c1, c8, c64, src, cwin, tmp, st, sp, dfc, lev, lag, w1s, w1, u1, pz,
    t2own, t2sib, t2m, t2, rown, rsib, rm, rr, fbuf, outb, send, recv, loc,
):
    p = lax.axis_index("tm")
    s = lax.axis_index("space")
    x = lax.rem(p, NX)
    g = lax.div(p, NX)
    z = lax.rem(g, NZ)
    y = lax.div(g, NZ)
    n_y = n_tm // (NX * NZ)
    plane = NX * NZ
    other = 1 - s
    row0 = pl.multiple_of(16 * s, 16)
    band = pl.ds(row0, 16)

    def dev(tm, space):
        return {"tm": tm, "space": space}

    barrier = pltpu.get_barrier_semaphore()

    def greet(tm, space):
        pl.semaphore_signal(barrier, inc=1, device_id=dev(tm, space), device_id_type=MESH)

    greet(p, other)

    @pl.when(p > 0)
    def _():
        greet(p - 1, 0)
        greet(p - 1, 1)

    for d in range(1, NX):
        greet(NX * g + lax.rem(x + d, NX), s)
    for d in range(1, NZ):
        greet(plane * y + NX * lax.rem(z + d, NZ) + x, s)
    for yy in range(n_y - 1):
        @pl.when(yy < y)
        def _():
            for xx in range(NX):
                greet(plane * yy + NX * z + xx, s)

    @pl.when(jnp.logical_and(x == 0, p > 0))
    def _():
        for d in range(1, NX + 1):
            greet(p - d, s)

    fields = (diffusion, velocity_x, velocity_y, source, initial)
    own = [pltpu.make_async_copy(f, fld.at[k, band, :], loc.at[k]) for k, f in enumerate(fields)]
    own.append(pltpu.make_async_copy(cpoints.at[pl.ds(0, 7)], cp.at[pl.ds(2, 7), band, :], loc.at[5]))
    for copy in own:
        copy.start()

    sends = 1 + (NX - 1) + (NZ - 1) + NX * (n_y - 1 - y)
    sends = sends + jnp.where(p < n_tm - 1, 2, 0)
    sends = sends + jnp.where(g < n_tm // NX - 1, 1, 0)
    pl.semaphore_wait(barrier, sends)

    def remote(src_ref, dst_ref, to, send_idx, recv_idx):
        return pltpu.make_async_remote_copy(
            src_ref=src_ref, dst_ref=dst_ref, send_sem=send.at[send_idx], recv_sem=recv.at[recv_idx],
            device_id=to, device_id_type=MESH,
        )

    sib = [
        remote(f, fld.at[k, band, :], dev(p, other), k, k) for k, f in enumerate(fields)
    ]
    sib.append(
        remote(cpoints.at[pl.ds(0, 7)], cp.at[pl.ds(2, 7), band, :], dev(p, other), 5, 5)
    )
    for copy in sib:
        copy.start()
    tail = cpoints.at[pl.ds(6, 2)]
    head = cp.at[pl.ds(0, 2), band, :]
    ahead = [remote(tail, head, dev(p + 1, ss), 6 + ss, 6 + s) for ss in range(2)]

    @pl.when(p < n_tm - 1)
    def _():
        for copy in ahead:
            copy.start()

    for copy in own[:5]:
        copy.wait()
    for copy in sib[:5]:
        copy.wait_recv()

    def rows_in(ref, k, slot):
        for c in range(C):
            for t in range(4):
                tmp[slot, c, pl.ds(8 * t, 8), :] = ref[k, pl.ds(8 * t, 8), COLS[c]]
        return [[tmp[slot, c, pl.ds(r, 8, stride=4), :] for r in range(R)] for c in range(C)]

    sub_row = sublanes()
    f_d, f_x, f_y, f_s, f_i = (rows_in(fld, k, k % 3) for k in range(5))
    store_state(src, f_s)
    store_state(fbuf, f_i)
    for c in range(C):
        for r in range(R):
            d, vx, vy = f_d[c][r], f_x[c][r], f_y[c][r]
            k0 = 4.0 * d + (jnp.abs(vx) + jnp.abs(vy))
            kl = d + jnp.maximum(vx, 0.0)
            kr = d - jnp.minimum(vx, 0.0)
            ku = d + jnp.maximum(vy, 0.0)
            kd = d - jnp.minimum(vy, 0.0)
            if r == 0:
                ku = jnp.where(sub_row == 0, 0.0, ku)
            if r == R - 1:
                kd = jnp.where(sub_row == 7, 0.0, kd)
            for ref, scale in ((c1, 1.0), (c8, 8.0), (c64, 64.0)):
                ref[0, c, r] = 1.0 - scale * k0
                for k, val in enumerate((kl, kr, ku, kd)):
                    ref[k + 1, c, r] = scale * val

    own[5].wait()
    sib[5].wait_recv()
    for k in range(7):
        store_state(st, rows_in(cp, k + 2, k % 3), k)

    def pair(i, carry):
        j = 2 * i
        a, b = full_steps(M, [load_state(st, j), load_state(st, j + 1)], c1, src)
        store_state(st, a, j + 7)
        store_state(st, b, j + 8)
        return carry

    lax.fori_loop(0, 6, pair, 0)

    @pl.when(p > 0)
    def _():
        for ss in range(2):
            remote(
                tail, cp.at[pl.ds(0, 2), pl.ds(16 * ss, 16), :], dev(p, other), 6, 6 + ss
            ).wait_recv()

    first_slab = p == 0

    @pl.when(p > 0)
    def _():
        for k in range(2):
            store_state(sp, rows_in(cp, k, k), k)

    @pl.when(first_slab)
    def _():
        for k in range(2):
            store_state(sp, load_state(fbuf), k)

    a, b, e = full_steps(M, [load_state(sp, 0), load_state(sp, 1), load_state(st, 12)], c1, src)
    store_state(sp, a, 2)
    store_state(sp, b, 3)
    store_state(st, e, 19)

    @pl.when(first_slab)
    def _():
        store_state(sp, load_state(fbuf), 2)

    a, b = full_steps(M, [load_state(sp, 2), load_state(sp, 3)], c1, src)
    store_state(dfc, sub(a, load_state(sp, 3)), 0)
    store_state(dfc, sub(b, load_state(st, 7)), 1)

    def defects(k, carry):
        store_state(dfc, sub(load_state(st, 12 + k), load_state(st, 6 + k)), k)
        return carry

    lax.fori_loop(2, M, defects, 0)

    def climb(k, v):
        return add(full_step([v], c8)[0], load_state(dfc, k))

    v = lax.fori_loop(1, M, climb, load_state(dfc, 0))
    store_state(lev, v)
    level = remote(lev, lag, dev(p + 1, s), 8, 8)

    @pl.when(p < n_tm - 1)
    def _():
        level.start()

    (v,) = full_steps(M, [v], c8)

    for c, tile in enumerate(window_tiles(v, s)):
        store_win(w1s, tile, c)
    to_x = []
    for d in range(1, NX):
        xx = lax.rem(x + d, NX)
        copy = remote(w1s.at[xx], w1.at[x], dev(NX * g + xx, s), 9 + d, 9 + x)
        copy.start()
        to_x.append(copy)
    store_win(w1, load_win(w1s, x), x)
    for k in range(5):
        tiles = window_tiles(load_state(c64, k), s)
        for r in range(R):
            mine = tiles[0][r]
            for c in range(1, C):
                mine = jnp.where(x == c, tiles[c][r], mine)
            cwin[k, r] = mine
    for d in range(1, NX):
        xx = lax.rem(x + d, NX)
        remote(w1s.at[xx], w1.at[xx], dev(NX * g + xx, s), 9, 9 + xx).wait_recv()
    acc = load_win(w1, 0)
    for i in range(1, NX):
        acc = add(win_step(acc, cwin), load_win(w1, i))
    store_win(u1, acc, z)

    to_z = []
    for d in (4, 3, 5, 2, 6, 1, 7) if NZ == 8 else range(1, NZ):
        zz = lax.rem(z + d, NZ)
        copy = remote(u1.at[z], u1.at[z], dev(plane * y + NX * zz + x, s), 13 + d, 13 + z)
        copy.start()
        to_z.append(copy)
    acc = [jnp.zeros(T, jnp.float32)] * R
    for zz in range(NZ):
        @pl.when(z == zz)
        def _():
            store_win(pz, acc)

        @pl.when(z != zz)
        def _():
            remote(u1.at[zz], u1.at[zz], dev(p, other), 13, 13 + zz).wait_recv()

        if zz > 0:
            acc = win_steps(NX, acc, cwin)
        acc = add(acc, load_win(u1, zz))
    store_win(t2own, acc)
    swap_t = remote(t2own, t2sib, dev(p, other), 21, 21)
    swap_t.start()

    acc = load_win(pz)
    store_win(rown, acc, 0)
    for i in range(NX):
        acc = add(win_step(acc, cwin), load_win(w1, i))
        store_win(rown, acc, i + 1)
    swap_r = remote(rown, rsib, dev(p, other), 38, 38)
    swap_r.start()

    swap_t.wait_recv()
    store_win(t2m, merged(load_win(t2own), load_win(t2sib), s))
    to_y = []
    for yy in range(1, n_y):
        for xx in range(NX):
            copy = remote(
                t2m, t2.at[y, x], dev(plane * yy + NX * z + xx, s),
                22 + NX * yy + xx, 22 + NX * y + x,
            )
            to_y.append((yy, copy))

            @pl.when(yy > y)
            def _():
                copy.start()

    swap_r.wait_recv()
    for i in range(NX + 1):
        store_win(rm, merged(load_win(rown, i), load_win(rsib, i), s), i)
    to_r = []
    for i in range(NX):
        there = NX * g + 1 + i
        copy = remote(rm.at[pl.ds(i, 2)], rr.at[x], dev(there, s), 39 + i, 39 + x)
        go = jnp.logical_and(x != i + 1, there < n_tm) if i == NX - 1 else x != i + 1
        to_r.append((go, copy))

        @pl.when(go)
        def _():
            copy.start()

        if i < NX - 1:
            @pl.when(x == i + 1)
            def _():
                store_win(rr, load_win(rm, i), x, 0)
                store_win(rr, load_win(rm, i + 1), x, 1)

    @pl.when(first_slab)
    def _():
        zero = [jnp.zeros(T, jnp.float32)] * R
        for c in range(C):
            store_win(rr, zero, c, 0)
            store_win(rr, zero, c, 1)
            store_win(lag, zero, c)

    q = jnp.maximum(p - 1, 0)
    xq = lax.rem(q, NX)
    zq = lax.rem(lax.div(q, NX), NZ)
    yq = lax.div(q, plane)
    store_state(fbuf, [[jnp.zeros(T, jnp.float32)] * R] * C)
    for yy in range(n_y - 1):
        @pl.when(yy < y)
        def _():
            for xx in range(NX):
                remote(t2m, t2.at[yy, xx], dev(p, other), 22, 22 + NX * yy + xx).wait_recv()

        @pl.when(yy < yq)
        def _():
            f = load_state(t2, yy)
            if yy > 0:
                (old,) = full_steps(plane, [load_state(fbuf)], c64)
                f = add(old, f)
            store_state(fbuf, f)

    trips = jnp.where(yq > 0, xq + NX * zq, 0)
    (f,) = full_steps(trips, [load_state(fbuf)], c64)

    @pl.when(p > 0)
    def _():
        level.wait_recv()
        for xx in range(NX):
            @pl.when(jnp.logical_or(x == 0, x != xx))
            def _():
                remote(rm.at[pl.ds(0, 2)], rr.at[xx], dev(p, other), 39, 39 + xx).wait_recv()

    e = [add(f[c], load_win(rr, c, 0)) for c in range(C)]
    (f,) = full_step([f], c64)
    last = [add(f[c], load_win(rr, c, 1)) for c in range(C)]
    last = add(last, load_state(lev))
    walker = add(load_state(lag), e)

    def emit(k, value):
        for c in range(C):
            for r in range(R):
                tmp[0, c, pl.ds(r, 8, stride=4), :] = value[c][r]
        for c in range(C):
            for t in range(2):
                outb[k, pl.ds(8 * t, 8), COLS[c]] = tmp[0, c, pl.ds(row0 + 8 * t, 8), :]

    def errors(k, v):
        v = add(full_step([v], c8)[0], load_state(dfc, k))
        store_state(st, add(v, load_state(st, k + 6)), k + 6)
        return v

    store_state(st, load_state(sp, 3), 6)
    lax.fori_loop(0, M - 1, errors, walker)
    store_state(st, add(last, load_state(st, 13)), 13)

    def emit_k(k, carry):
        emit(k, load_state(st, k + 6))
        return carry

    lax.fori_loop(0, M, emit_k, 0)
    done = pltpu.make_async_copy(outb, out, loc.at[6])
    done.start()

    for copy in sib:
        copy.wait_send()

    @pl.when(p < n_tm - 1)
    def _():
        for copy in ahead:
            copy.wait_send()
        level.wait_send()

    for copy in to_x + to_z + [swap_t, swap_r]:
        copy.wait_send()
    for yy, copy in to_y:
        @pl.when(yy > y)
        def _():
            copy.wait_send()

    for go, copy in to_r:
        @pl.when(go)
        def _():
            copy.wait_send()

    done.wait()


def body(n_tm, *args):
    f32 = jnp.float32

    def vmem(*shape):
        return pltpu.VMEM(shape, f32)

    state = STATE
    scratch = [
        vmem(9, 32, 512), vmem(5, 32, 512),
        vmem(5, *state), vmem(5, *state), vmem(5, *state), vmem(*state), vmem(5, *WIN),
        vmem(3, C, 32, 128), vmem(20, *state), vmem(4, *state), vmem(M, *state),
        vmem(*state), vmem(*state),
        vmem(NX, *WIN), vmem(NX, *WIN), vmem(NZ, *WIN), vmem(*WIN),
        vmem(*WIN), vmem(*WIN), vmem(*WIN), vmem(max(n_tm // (NX * NZ) - 1, 1), C, *WIN),
        vmem(NX + 1, *WIN), vmem(NX + 1, *WIN), vmem(NX + 1, *WIN), vmem(C, 2, *WIN),
        vmem(*state), vmem(M, 16, 512),
        pltpu.SemaphoreType.DMA((43,)), pltpu.SemaphoreType.DMA((43,)), pltpu.SemaphoreType.DMA((7,)),
    ]
    return pl.pallas_call(
        functools.partial(kernel, n_tm),
        out_shape=jax.ShapeDtypeStruct(args[0].shape, f32),
        in_specs=[pl.BlockSpec(memory_space=pl.ANY)] * 6,
        out_specs=pl.BlockSpec(memory_space=pl.ANY),
        scratch_shapes=scratch,
        compiler_params=pltpu.CompilerParams(
            collective_id=0, has_side_effects=True, vmem_limit_bytes=32 * 1024 * 1024
        ),
    )(*args)


def solution(mesh):
    placed = (
        P("tm", "space", None),
        P("space", None),
        P("space", None),
        P("space", None),
        P("space", None),
        P("space", None),
    )
    return jax.shard_map(
        functools.partial(body, mesh.shape["tm"]),
        mesh=mesh, in_specs=placed, out_specs=P("tm", "space", None), check_vma=False,
    )
```

time: 541 us -> 54.4 us (0.10); the launches traced: 531 us -> 54 us
  starting transfers between devices: 182 us -> 0 us
  waiting for transfers between devices: 158 us -> 0 us
  other arithmetic: 140 us -> 0 us
  Pallas kernels: 0 us -> 48.5 us
  local copies, waits for them, and re-layouts: 27.9 us -> 5.44 us
  between operations: 14.7 us -> 0.02 us
    ppermute x83 -> x0, starting transfers between devices: 182 us -> none  [the longest x40 124 us: with_halo(): after = lax.ppermute(initial, axis, down)]
    select_n x130 -> x0, other arithmetic: 123 us -> none  [the longest x127 122 us: coarse_step(): retained = jnp.where(step_idx == slab_idx - 1, current, retained)]
    all_gather x1 -> x0, waiting for transfers between devices: 114 us -> none  [body(): gathered = lax.all_gather(rows_all, 'tm', axis=0, tiled=True)]
    pallas_call x0 -> x1, Pallas kernels: none -> 48.5 us  [body(): pl.pallas_call(functools.partial(kernel, n_tm), out_shape=jax.ShapeDtypeS...]
    ppermute x83 -> x0, waiting for transfers between devices: 43.6 us -> none  [the longest x40 26.1 us: with_halo(): after = lax.ppermute(initial, axis, down)]
    slice x370 -> x0, local copies, waits for them, and re-layouts: 27.9 us -> none  [the longest x267 20.1 us: stencil(): right_col = jnp.roll(centre, -1, axis=-1)]
    add x33 -> x0, other arithmetic: 13.9 us -> none  [the longest x15 6.48 us: relax_fine(): states = band_step(states, coeffs, 1.0) + source]
  transfers between devices with their start and end apart: 84 -> 0, of which waited for: 41 -> 0; matrix products, arithmetic and copies ran while one was open for 2% -> 0% of each run, Pallas kernels for 0% -> 0%
where the time goes in v1:
time: 54.4 us; the launch traced here: 54 us
  Pallas kernels  48.5 us (89%)
  local copies, waits for them, and re-layouts  5.44 us (10%)
    pallas_call x1, Pallas kernels, body(): pl.pallas_call(functools.partial(kernel, n_tm), out_shape=jax.ShapeDtypeS...  48.5 us
    unnamed x13, local copies, waits for them, and re-layouts  5.44 us

profile of v1, /device:TPU:25, one launch (start us, length us, event | category | flops | bytes accessed | tf_op | source)
XLA Modules:
  0.0 54.0 jit_solution(3658882563170511639)
XLA Ops:
  0.0 0.0 copy-start
  0.0 0.9 %copy-done = f32[8,16,512]{2,1,0:T(8,128)S(1)} copy-done((f32[8,16,512]{2,1,0:T(8,128)S(1)}, f32[8,16,512]{2,1,0:T(8,128)}, u32[]{:S(2)}) %copy-start) | copy-done | bytes 262168
  1.0 0.0 copy-start.1
  1.0 0.8 %copy-done.1 = f32[16,512]{1,0:T(8,128)S(1)} copy-done((f32[16,512]{1,0:T(8,128)S(1)}, f32[16,512]{1,0:T(8,128)}, u32[]{:S(2)}) %copy-start.1) | copy-done | bytes 32792
  1.7 0.0 copy-start.2
  1.7 0.8 %copy-done.2 = f32[16,512]{1,0:T(8,128)S(1)} copy-done((f32[16,512]{1,0:T(8,128)S(1)}, f32[16,512]{1,0:T(8,128)}, u32[]{:S(2)}) %copy-start.2) | copy-done | bytes 32792
  2.5 0.0 copy-start.3
  2.5 0.8 %copy-done.3 = f32[16,512]{1,0:T(8,128)S(1)} copy-done((f32[16,512]{1,0:T(8,128)S(1)}, f32[16,512]{1,0:T(8,128)}, u32[]{:S(2)}) %copy-start.3) | copy-done | bytes 32792
  3.2 0.0 copy-start.4
  3.2 0.8 %copy-done.4 = f32[16,512]{1,0:T(8,128)S(1)} copy-done((f32[16,512]{1,0:T(8,128)S(1)}, f32[16,512]{1,0:T(8,128)}, u32[]{:S(2)}) %copy-start.4) | copy-done | bytes 32792
  4.0 0.0 copy-start.5
  4.0 0.8 %copy-done.5 = f32[16,512]{1,0:T(8,128)S(1)} copy-done((f32[16,512]{1,0:T(8,128)S(1)}, f32[16,512]{1,0:T(8,128)}, u32[]{:S(2)}) %copy-start.5) | copy-done | bytes 32792
  4.7 48.5 %shard_map.64 = f32[8,16,512]{2,1,0:T(8,128)S(1)} custom-call(f32[8,16,512]{2,1,0:T(8,128)S(1)} %copy-done, f32[16,512]{1,0:T(8,128)S(1)} %copy-done.1, f32[16,512]{1,0:T(8,128)S(1)} %copy-done.2, f32[16,512]{1,0:T(8,128)S(1)} %copy-done.3, f32[16,512]{1,0:T(8,128)S(1)} %copy-done.4, f32[16,512]{1,0:T(8,128)S(1)} %copy-done.5), custom_call_target="tpu_custom_call" | custom-call | tf_op jit(solution)/shard_map/pallas_call | solution.py:519
  53.3 0.7 %copy.8 = f32[8,16,512]{2,1,0:T(8,128)} copy(f32[8,16,512]{2,1,0:T(8,128)S(1)} %shard_map.64) | data formatting | bytes 524288
Async XLA Ops:
  0.0 0.9 %copy-start = (f32[8,16,512]{2,1,0:T(8,128)S(1)}, f32[8,16,512]{2,1,0:T(8,128)}, u32[]{:S(2)}) copy-start(f32[8,16,512]{2,1,0:T(8,128)} %cpoints.1) | copy-start | bytes 786436
  1.0 0.8 %copy-start.1 = (f32[16,512]{1,0:T(8,128)S(1)}, f32[16,512]{1,0:T(8,128)}, u32[]{:S(2)}) copy-start(f32[16,512]{1,0:T(8,128)} %initial.1) | copy-start | bytes 98308
  1.7 0.8 %copy-start.2 = (f32[16,512]{1,0:T(8,128)S(1)}, f32[16,512]{1,0:T(8,128)}, u32[]{:S(2)}) copy-start(f32[16,512]{1,0:T(8,128)} %diffusion.1) | copy-start | bytes 98308
  2.5 0.8 %copy-start.3 = (f32[16,512]{1,0:T(8,128)S(1)}, f32[16,512]{1,0:T(8,128)}, u32[]{:S(2)}) copy-start(f32[16,512]{1,0:T(8,128)} %velocity_x.1) | copy-start | bytes 98308
  3.2 0.8 %copy-start.4 = (f32[16,512]{1,0:T(8,128)S(1)}, f32[16,512]{1,0:T(8,128)}, u32[]{:S(2)}) copy-start(f32[16,512]{1,0:T(8,128)} %velocity_y.1) | copy-start | bytes 98308
  4.0 0.8 %copy-start.5 = (f32[16,512]{1,0:T(8,128)S(1)}, f32[16,512]{1,0:T(8,128)}, u32[]{:S(2)}) copy-start(f32[16,512]{1,0:T(8,128)} %source.1) | copy-start | bytes 98308

commit v2 on v1

v2 whole, which is shorter than its diff:
```python
import functools

import jax
import jax.numpy as jnp
from jax import lax
from jax.experimental import pallas as pl
from jax.experimental.pallas import tpu as pltpu
from jax.sharding import PartitionSpec as P

M = 8
NX = 4
NZ = 8
C = 4
R = 4
T = (8, 128)
W = 128 * C
NY = 8 * R
MESH = pl.DeviceIdType.MESH
BF16 = jnp.bfloat16
F32 = jnp.float32


def tile(ref, lead, r, c):
    return ref[(*lead, pl.ds(8 * r, 8), pl.ds(128 * c, 128))]


def load_state(ref, *lead, columns=C):
    return [[tile(ref, lead, r, c) for r in range(R)] for c in range(columns)]


def store_state(ref, v, *lead):
    for c, column in enumerate(v):
        for r in range(R):
            ref[(*lead, pl.ds(8 * r, 8), pl.ds(128 * c, 128))] = column[r]


def load_win(ref, *lead):
    return load_state(ref, *lead, columns=1)[0]


def store_win(ref, v, *lead):
    store_state(ref, [v], *lead)


def add(a, b):
    if isinstance(a, list):
        return [add(x, y) for x, y in zip(a, b)]
    return a + b


def sub(a, b):
    if isinstance(a, list):
        return [sub(x, y) for x, y in zip(a, b)]
    return a - b


def iota(shape, dim):
    return lax.broadcasted_iota(jnp.int32, shape, dim)


def at_row(column, r, di):
    carry, index = divmod(r + di, R)
    x = column[index]
    return x if carry == 0 else pltpu.roll(x, (-carry) % 8, 0)


def beside(v, width):
    ext = {c: v[c] for c in range(C)}
    for j in range(1, width + 1):
        ext[-j] = [pltpu.roll(x, 1, 1) for x in v[C - j]]
        ext[C - 1 + j] = [pltpu.roll(x, 127, 1) for x in v[j - 1]]
    return ext


def advance(states, coef, first, count, source=None):
    exts = [beside(v, count) for v in states]
    for j in range(count):
        width = count - 1 - j
        news = [{} for _ in exts]
        for c in range(-width, C + width):
            for n in news:
                n[c] = []
            for r in range(R):
                k0, kl, kr, ku, kd = (tile(coef, (k,), r, c - first) for k in range(5))
                plus = None if source is None else tile(source, (), r, c)
                for n, e in zip(news, exts):
                    new = (k0 * e[c][r] + kl * e[c - 1][r]) + (kr * e[c + 1][r] + ku * at_row(e[c], r, -1))
                    new = new + kd * at_row(e[c], r, 1)
                    n[c].append(new if plus is None else new + plus)
        exts = news
    return [[e[c] for c in range(C)] for e in exts]


def relax(states, coef, source):
    return lax.fori_loop(0, M, lambda _, s: advance(s, coef, 0, 1, source), states)


def move(v, coef, times, count=2, unroll=1):
    def some(_, s):
        for _ in range(unroll):
            s = advance(s, coef, -1, count)
        return s

    return lax.fori_loop(0, times, some, [v])[0]


ONE = [(0, 0), (0, -1), (0, 1), (-1, 0), (1, 0)]


def sums(a, b):
    out = []
    for d in a:
        for e in b:
            f = (d[0] + e[0], d[1] + e[1])
            if f not in out:
                out.append(f)
    return out


TWO = sums(ONE, ONE)
FOUR = sums(TWO, TWO)


def along(v, dj):
    return v if dj == 0 else [pltpu.roll(x, (-dj) % 128, 1) for x in v]


def win_apply(v, coef, offsets):
    moved = {dj: along(v, dj) for dj in sorted({d[1] for d in offsets})}
    out = []
    for r in range(R):
        parts = [None] * 4
        for n, (di, dj) in enumerate(offsets):
            term = tile(coef, (n,), r, 0) * at_row(moved[dj], r, di)
            parts[n % 4] = term if parts[n % 4] is None else parts[n % 4] + term
        out.append((parts[0] + parts[1]) + (parts[2] + parts[3]))
    return out


def compose(out, a, a_offsets, b, b_offsets, out_offsets):
    seen = set()
    for dj in sorted({d[1] for d in a_offsets}):
        for n, e in enumerate(b_offsets):
            moved = along(load_win(b, n), dj)
            for m, d in enumerate(a_offsets):
                if d[1] != dj:
                    continue
                k = out_offsets.index((d[0] + e[0], d[1] + e[1]))
                for r in range(R):
                    term = tile(a, (m,), r, 0) * at_row(moved, r, d[0])
                    if k in seen:
                        term = term + tile(out, (k,), r, 0)
                    out[k, pl.ds(8 * r, 8), :] = term
                seen.add(k)


def permuted(x, matrix):
    high = x.astype(BF16)
    rest = x - high.astype(F32)
    mid = rest.astype(BF16)
    low = (rest - mid.astype(F32)).astype(BF16)
    a, b, c = (jnp.dot(part, matrix, preferred_element_type=F32) for part in (high, mid, low))
    return (a + b) + c


def selector(row_of_column):
    return jnp.where(iota((W, W), 0) == row_of_column, 1.0, 0.0).astype(BF16)


def inner_place(column):
    return 128 * lax.rem(column, C) + lax.div(column, C)


def merged(own, other, band):
    lane = iota(T, 1)
    low = band == 0
    out = []
    for a, b in zip(own, other):
        w0, w1 = jnp.where(low, a, b), jnp.where(low, b, a)
        out.append(jnp.where(lane < 64, pltpu.roll(w0, 96, 1), pltpu.roll(w1, 32, 1)))
    return out


def kernel(
    n_tm, cpoints, initial, diffusion, velocity_x, velocity_y, source, out,
    raw, perm_in, perm_win, perm_out, c1, c8, c64, src, init, cw1, cw2, cw4, cwide, rows, cpi, rel, dfc,
    lev, lag, w1s, w1, u1, pz, t2own, t2sib, t2m, t2, rown, rsib, rm, rr, rri, t2i, fbuf, outi, outb,
    send, recv, loc,
):
    p = lax.axis_index("tm")
    s = lax.axis_index("space")
    x = lax.rem(p, NX)
    g = lax.div(p, NX)
    z = lax.rem(g, NZ)
    y = lax.div(g, NZ)
    n_y = n_tm // (NX * NZ)
    plane = NX * NZ
    other = 1 - s
    row0 = pl.multiple_of(16 * s, 16)
    first_slab = p == 0

    def dev(tm, space):
        return {"tm": tm, "space": space}

    def cols(c):
        return pl.ds(pl.multiple_of(128 * c, 128), 128)

    barrier = pltpu.get_barrier_semaphore()

    def greet(tm, space):
        pl.semaphore_signal(barrier, inc=1, device_id=dev(tm, space), device_id_type=MESH)

    for d in (4, 3, 5, 2, 6, 1, 7):
        greet(plane * y + NX * lax.rem(z + d, NZ) + x, s)
    for yy in range(n_y - 1):
        @pl.when(yy < y)
        def _():
            for xx in range(NX):
                greet(plane * yy + NX * z + xx, s)

    @pl.when(p > 0)
    def _():
        greet(p - 1, 0)
        greet(p - 1, 1)

    for d in (2, 1, 3):
        greet(NX * g + lax.rem(x + d, NX), s)

    @pl.when(jnp.logical_and(x == 0, p > 0))
    def _():
        for d in range(1, NX + 1):
            greet(p - d, s)

    greet(p, other)

    fields = (diffusion, velocity_x, velocity_y, source, initial)
    own = [pltpu.make_async_copy(f, raw.at[k, pl.ds(row0, 16), :], loc.at[k]) for k, f in enumerate(fields)]
    own.append(
        pltpu.make_async_copy(cpoints.at[pl.ds(0, 7)], raw.at[pl.ds(5, 7), pl.ds(row0, 16), :], loc.at[5])
    )
    for copy in own:
        copy.start()

    sends = 1 + (NX - 1) + (NZ - 1) + NX * (n_y - 1 - y)
    sends = sends + jnp.where(p < n_tm - 1, 2, 0)
    sends = sends + jnp.where(g < n_tm // NX - 1, 1, 0)
    pl.semaphore_wait(barrier, sends)

    def remote(src_ref, dst_ref, to, send_idx, recv_idx):
        return pltpu.make_async_remote_copy(
            src_ref=src_ref, dst_ref=dst_ref, send_sem=send.at[send_idx], recv_sem=recv.at[recv_idx],
            device_id=to, device_id_type=MESH,
        )

    tail = cpoints.at[pl.ds(6, 2)]
    ahead = [
        remote(tail, raw.at[pl.ds(12, 2), pl.ds(row0, 16), :], dev(p + 1, ss), 6 + ss, 6 + s) for ss in range(2)
    ]

    @pl.when(p < n_tm - 1)
    def _():
        for copy in ahead:
            copy.start()

    sib = [
        remote(f, raw.at[k, pl.ds(row0, 16), :], dev(p, other), k, k) for k, f in enumerate(fields)
    ]
    sib.append(
        remote(cpoints.at[pl.ds(0, 7)], raw.at[pl.ds(5, 7), pl.ds(row0, 16), :], dev(p, other), 5, 5)
    )
    for copy in sib:
        copy.start()

    line = iota((1, W), 1)
    perm_in[...] = selector(C * lax.rem(line, 128) + lax.div(line, 128))

    for copy in own:
        copy.wait()
    for copy in sib:
        copy.wait_recv()

    def inward(first, count, emit):
        moved = permuted(raw[pl.ds(first, count)].reshape(count * NY, W), perm_in[...])
        for c in range(C):
            rows[c, pl.ds(0, count * NY), :] = moved[:, 128 * c : 128 * (c + 1)]
        for k in range(count):
            emit(k, [[rows[c, pl.ds(NY * k + r, 8, stride=R), :] for r in range(R)] for c in range(C)])

    got = {}

    def keep(k, v):
        if k < 3:
            got[k] = v
        elif k == 3:
            store_state(src, v)
        elif k == 4:
            store_state(init, v)
        else:
            store_state(cpi, v, k - 3)

    inward(0, 12, keep)

    sub_row = iota(T, 0)
    for c in range(C):
        for r in range(R):
            d, vx, vy = (got[k][c][r] for k in range(3))
            k0 = 4.0 * d + (jnp.abs(vx) + jnp.abs(vy))
            kl = d + jnp.maximum(vx, 0.0)
            kr = d - jnp.minimum(vx, 0.0)
            ku = d + jnp.maximum(vy, 0.0)
            kd = d - jnp.minimum(vy, 0.0)
            if r == 0:
                ku = jnp.where(sub_row == 0, 0.0, ku)
            if r == R - 1:
                kd = jnp.where(sub_row == 7, 0.0, kd)
            here = (pl.ds(8 * r, 8), pl.ds(128 * c, 128))
            wide = (pl.ds(8 * r, 8), pl.ds(128 * (c + 1), 128))
            for ref, scale, at in ((c1, 1.0, here), (c8, 8.0, wide), (c64, 64.0, wide)):
                ref[(0, *at)] = 1.0 - scale * k0
                for k, val in enumerate((kl, kr, ku, kd)):
                    ref[(k + 1, *at)] = scale * val

    first = relax([load_state(cpi, k) for k in range(2, 9)], c1, src)
    for k, v in enumerate(first):
        store_state(rel, v, k + 2)

    @pl.when(p > 0)
    def _():
        for ss in range(2):
            remote(
                tail, raw.at[pl.ds(12, 2), pl.ds(16 * ss, 16), :], dev(p, other), 6, 6 + ss
            ).wait_recv()

        inward(12, 2, lambda k, v: store_state(cpi, v, k))

    @pl.when(first_slab)
    def _():
        for k in range(2):
            store_state(cpi, load_state(init), k)

    second = relax(
        [load_state(cpi, 0), load_state(cpi, 1)] + [load_state(rel, k) for k in range(2, 8)], c1, src
    )
    for k in range(2):
        store_state(rel, second[k], k)
    for k in range(2, M):
        store_state(dfc, sub(second[k], load_state(rel, k + 1)), k)

    @pl.when(first_slab)
    def _():
        store_state(rel, load_state(init), 0)

    third = relax([load_state(rel, 0), load_state(rel, 1)], c1, src)
    for k in range(2):
        store_state(dfc, sub(third[k], load_state(rel, k + 1)), k)

    for ref in (c8, c64):
        for k in range(5):
            for r in range(R):
                ref[k, pl.ds(8 * r, 8), pl.ds(0, 128)] = pltpu.roll(tile(ref, (k,), r, C), 1, 1)
                ref[k, pl.ds(8 * r, 8), pl.ds(128 * (C + 1), 128)] = pltpu.roll(tile(ref, (k,), r, 1), 127, 1)

    def climb(k, v):
        return add(advance([v], c8, -1, 1)[0], load_state(dfc, k))

    v = lax.fori_loop(1, M, climb, load_state(dfc, 0))
    store_state(lev, v)
    level = remote(lev, lag, dev(p + 1, s), 8, 8)
    v = move(v, c8, M // 2)
    store_state(fbuf, v)

    perm_win[...] = selector(
        inner_place(lax.rem(128 * lax.div(line, 128) + 64 * s + (W - 32) + lax.rem(line, 128), W))
    )
    w1s[...] = permuted(fbuf[...], perm_win[...])
    to_x = []
    for d in (2, 1, 3):
        xx = lax.rem(x + d, NX)
        copy = remote(w1s.at[:, cols(xx)], w1.at[x], dev(NX * g + xx, s), 9 + d, 9 + x)
        copy.start()
        to_x.append(copy)

    @pl.when(p < n_tm - 1)
    def _():
        level.start()

    store_win(w1, [w1s[pl.ds(8 * r, 8), cols(x)] for r in range(R)], x)

    cwide[...] = permuted(c64[:, :, pl.ds(128, W)].reshape(5 * NY, W), perm_win[...])
    for k in range(5):
        cw1[k] = cwide[pl.ds(NY * k, NY), cols(x)]
    compose(cw2, cw1, ONE, cw1, ONE, TWO)
    compose(cw4, cw2, TWO, cw2, TWO, FOUR)
    perm_out[...] = selector(inner_place(line))

    for d in range(1, NX):
        xx = lax.rem(x + d, NX)
        remote(w1s.at[:, cols(xx)], w1.at[xx], dev(NX * g + xx, s), 9, 9 + xx).wait_recv()
    a = add(win_apply(load_win(w1, 0), cw1, ONE), load_win(w1, 1))
    b = add(win_apply(load_win(w1, 2), cw1, ONE), load_win(w1, 3))
    store_win(u1, add(win_apply(a, cw2, TWO), b), z)

    to_z = []
    for d in (4, 3, 5, 2, 6, 1, 7):
        zz = lax.rem(z + d, NZ)
        copy = remote(u1.at[z], u1.at[z], dev(plane * y + NX * zz + x, s), 13 + d, 13 + z)
        copy.start()
        to_z.append(copy)

    pz[...] = jnp.zeros_like(pz)

    @pl.when(z != 0)
    def _():
        remote(u1.at[0], u1.at[0], dev(p, other), 13, 13).wait_recv()

    def ascend(zz, acc):
        @pl.when(z == zz)
        def _():
            store_win(pz, acc)

        @pl.when(z != zz)
        def _():
            remote(u1.at[zz], u1.at[zz], dev(p, other), 13, 13 + zz).wait_recv()

        return add(win_apply(acc, cw4, FOUR), load_win(u1, zz))

    store_win(t2own, lax.fori_loop(1, NZ, ascend, load_win(u1, 0)))
    swap_t = remote(t2own, t2sib, dev(p, other), 21, 21)
    swap_t.start()

    acc = load_win(pz)
    store_win(rown, acc, 0)
    for i in range(NX):
        acc = add(win_apply(acc, cw1, ONE), load_win(w1, i))
        store_win(rown, acc, i + 1)
    swap_r = remote(rown, rsib, dev(p, other), 38, 38)
    swap_r.start()

    swap_t.wait_recv()
    store_win(t2m, merged(load_win(t2own), load_win(t2sib), s))
    to_y = []
    for yy in range(1, n_y):
        for xx in range(NX):
            copy = remote(
                t2m, t2.at[y, :, cols(x)], dev(plane * yy + NX * z + xx, s),
                22 + NX * yy + xx, 22 + NX * y + x,
            )
            to_y.append((yy, copy))

            @pl.when(yy > y)
            def _():
                copy.start()

    swap_r.wait_recv()
    for i in range(NX + 1):
        store_win(rm, merged(load_win(rown, i), load_win(rsib, i), s), i)
    to_r = []
    for i in range(NX):
        there = NX * g + 1 + i
        copy = remote(rm.at[pl.ds(i, 2)], rr.at[:, :, cols(x)], dev(there, s), 39 + i, 39 + x)
        go = jnp.logical_and(x != i + 1, there < n_tm) if i == NX - 1 else x != i + 1
        to_r.append((go, copy))

        @pl.when(go)
        def _():
            copy.start()

        if i < NX - 1:
            @pl.when(x == i + 1)
            def _():
                for j in range(2):
                    rr[j, :, cols(x)] = rm[i + j]

    @pl.when(first_slab)
    def _():
        rr[...] = jnp.zeros_like(rr)
        lag[...] = jnp.zeros_like(lag)

    @pl.when(p > 0)
    def _():
        level.wait_recv()
        for xx in range(NX):
            @pl.when(jnp.logical_or(x == 0, x != xx))
            def _():
                remote(
                    rm.at[pl.ds(0, 2)], rr.at[:, :, cols(xx)], dev(p, other), 39, 39 + xx
                ).wait_recv()

    rri[...] = permuted(rr[...].reshape(2 * NY, W), perm_in[...]).reshape(2, NY, W)

    q = jnp.maximum(p - 1, 0)
    n = lax.rem(q, plane)
    yq = lax.div(q, plane)
    fbuf[...] = jnp.zeros_like(fbuf)
    for yy in range(n_y - 1):
        @pl.when(yy < y)
        def _():
            for xx in range(NX):
                remote(t2m, t2.at[yy, :, cols(xx)], dev(p, other), 22, 22 + NX * yy + xx).wait_recv()

    for yy in range(n_y - 1):
        @pl.when(yy < yq)
        def _():
            t2i[...] = permuted(t2[yy], perm_in[...])
            f = load_state(t2i)
            if yy > 0:
                f = add(move(load_state(fbuf), c64, plane // 4, 2, 2), f)
            store_state(fbuf, f)

    n = jnp.where(yq > 0, n, 0)
    f = move(load_state(fbuf), c64, lax.div(n, 2))
    f = move(f, c64, lax.rem(n, 2), 1)
    e = add(f, load_state(rri, 0))
    (f,) = advance([f], c64, -1, 1)
    last = add(add(f, load_state(rri, 1)), load_state(lev))

    def emit(k, value):
        for c in range(C):
            for r in range(R):
                rows[c, pl.ds(r, 8, stride=R), :] = value[c][r]
        for c in range(C):
            for t in range(2):
                outi[k, pl.ds(8 * t, 8), pl.ds(128 * c, 128)] = rows[c, pl.ds(pl.multiple_of(row0 + 8 * t, 8), 8), :]

    emit(M - 1, add(last, load_state(rel, M)))

    def errors(k, v):
        v = add(advance([v], c8, -1, 1)[0], load_state(dfc, k))
        emit(k, add(v, load_state(rel, k + 1)))
        return v

    lax.fori_loop(0, M - 1, errors, add(load_state(lag), e))
    outb[...] = permuted(outi[...].reshape(M * 16, W), perm_out[...]).reshape(M, 16, W)
    done = pltpu.make_async_copy(outb, out, loc.at[6])
    done.start()

    for copy in sib:
        copy.wait_send()

    @pl.when(p < n_tm - 1)
    def _():
        for copy in ahead:
            copy.wait_send()
        level.wait_send()

    for copy in to_x + to_z + [swap_t, swap_r]:
        copy.wait_send()
    for yy, copy in to_y:
        @pl.when(yy > y)
        def _():
            copy.wait_send()

    for go, copy in to_r:
        @pl.when(go)
        def _():
            copy.wait_send()

    done.wait()


def body(n_tm, *args):
    def vmem(*shape, dtype=F32):
        return pltpu.VMEM(shape, dtype)

    def state(*lead):
        return vmem(*lead, NY, W)

    def window(*lead):
        return vmem(*lead, NY, 128)

    square = vmem(W, W, dtype=BF16)
    scratch = [
        state(14), square, square, square,
        state(5), vmem(5, NY, W + 256), vmem(5, NY, W + 256), state(), state(),
        window(len(ONE)), window(len(TWO)), window(len(FOUR)), vmem(5 * NY, W),
        vmem(C, 12 * NY, 128), state(9), state(9), state(M),
        state(), state(), state(), window(NX), window(NZ), window(),
        window(), window(), window(), state(max(n_tm // (NX * NZ) - 1, 1)),
        window(NX + 1), window(NX + 1), window(NX + 1), state(2), state(2), state(),
        state(), vmem(M, 16, W), vmem(M, 16, W),
        pltpu.SemaphoreType.DMA((43,)), pltpu.SemaphoreType.DMA((43,)), pltpu.SemaphoreType.DMA((7,)),
    ]
    return pl.pallas_call(
        functools.partial(kernel, n_tm),
        out_shape=jax.ShapeDtypeStruct(args[0].shape, F32),
        in_specs=[pl.BlockSpec(memory_space=pltpu.HBM)] * 6,
        out_specs=pl.BlockSpec(memory_space=pltpu.HBM),
        scratch_shapes=scratch,
        compiler_params=pltpu.CompilerParams(
            collective_id=0, has_side_effects=True, vmem_limit_bytes=40 * 1024 * 1024
        ),
    )(*args)


def solution(mesh):
    placed = (
        P("tm", "space", None),
        P("space", None),
        P("space", None),
        P("space", None),
        P("space", None),
        P("space", None),
    )
    return jax.shard_map(
        functools.partial(body, mesh.shape["tm"]),
        mesh=mesh, in_specs=placed, out_specs=P("tm", "space", None), check_vma=False,
    )
```

time: 54.4 us -> 48.6 us (0.89)
  Pallas kernels: 48.5 us -> 42.7 us
    pallas_call x1, Pallas kernels: 48.5 us -> 42.7 us  [body(): pl.pallas_call(functools.partial(kernel, n_tm), out_shape=jax.ShapeDtypeS...]
where the time goes in v2:
time: 48.6 us; the launch traced here: 48.1 us
  Pallas kernels  42.7 us (88%)
  local copies, waits for them, and re-layouts  5.44 us (11%)
    pallas_call x1, Pallas kernels, body(): pl.pallas_call(functools.partial(kernel, n_tm), out_shape=jax.ShapeDtypeS...  42.7 us
    unnamed x13, local copies, waits for them, and re-layouts  5.44 us

profile of v2, /device:TPU:25, one launch (start us, length us, event | category | flops | bytes accessed | tf_op | source)
XLA Modules:
  0.0 48.1 jit_solution(1639476076233822644)
XLA Ops:
  0.0 0.0 copy-start
  0.0 0.9 %copy-done = f32[8,16,512]{2,1,0:T(8,128)S(1)} copy-done((f32[8,16,512]{2,1,0:T(8,128)S(1)}, f32[8,16,512]{2,1,0:T(8,128)}, u32[]{:S(2)}) %copy-start) | copy-done | bytes 262168
  1.0 0.0 copy-start.1
  1.0 0.8 %copy-done.1 = f32[16,512]{1,0:T(8,128)S(1)} copy-done((f32[16,512]{1,0:T(8,128)S(1)}, f32[16,512]{1,0:T(8,128)}, u32[]{:S(2)}) %copy-start.1) | copy-done | bytes 32792
  1.7 0.0 copy-start.2
  1.7 0.8 %copy-done.2 = f32[16,512]{1,0:T(8,128)S(1)} copy-done((f32[16,512]{1,0:T(8,128)S(1)}, f32[16,512]{1,0:T(8,128)}, u32[]{:S(2)}) %copy-start.2) | copy-done | bytes 32792
  2.5 0.0 copy-start.3
  2.5 0.8 %copy-done.3 = f32[16,512]{1,0:T(8,128)S(1)} copy-done((f32[16,512]{1,0:T(8,128)S(1)}, f32[16,512]{1,0:T(8,128)}, u32[]{:S(2)}) %copy-start.3) | copy-done | bytes 32792
  3.2 0.0 copy-start.4
  3.2 0.8 %copy-done.4 = f32[16,512]{1,0:T(8,128)S(1)} copy-done((f32[16,512]{1,0:T(8,128)S(1)}, f32[16,512]{1,0:T(8,128)}, u32[]{:S(2)}) %copy-start.4) | copy-done | bytes 32792
  4.0 0.0 copy-start.5
  4.0 0.8 %copy-done.5 = f32[16,512]{1,0:T(8,128)S(1)} copy-done((f32[16,512]{1,0:T(8,128)S(1)}, f32[16,512]{1,0:T(8,128)}, u32[]{:S(2)}) %copy-start.5) | copy-done | bytes 32792
  4.7 42.7 %shard_map.64 = f32[8,16,512]{2,1,0:T(8,128)S(1)} custom-call(f32[8,16,512]{2,1,0:T(8,128)S(1)} %copy-done, f32[16,512]{1,0:T(8,128)S(1)} %copy-done.1, f32[16,512]{1,0:T(8,128)S(1)} %copy-done.2, f32[16,512]{1,0:T(8,128)S(1)} %copy-done.3, f32[16,512]{1,0:T(8,128)S(1)} %copy-done.4, f32[16,512]{1,0:T(8,128)S(1)} %copy-done.5), custom_call_target="tpu_custom_call" | custom-call | tf_op jit(solution)/shard_map/pallas_call | solution.py:583
  47.4 0.7 %copy.8 = f32[8,16,512]{2,1,0:T(8,128)} copy(f32[8,16,512]{2,1,0:T(8,128)S(1)} %shard_map.64) | data formatting | bytes 524288
Async XLA Ops:
  0.0 0.9 %copy-start = (f32[8,16,512]{2,1,0:T(8,128)S(1)}, f32[8,16,512]{2,1,0:T(8,128)}, u32[]{:S(2)}) copy-start(f32[8,16,512]{2,1,0:T(8,128)} %cpoints.1) | copy-start | bytes 786436
  1.0 0.8 %copy-start.1 = (f32[16,512]{1,0:T(8,128)S(1)}, f32[16,512]{1,0:T(8,128)}, u32[]{:S(2)}) copy-start(f32[16,512]{1,0:T(8,128)} %initial.1) | copy-start | bytes 98308
  1.7 0.8 %copy-start.2 = (f32[16,512]{1,0:T(8,128)S(1)}, f32[16,512]{1,0:T(8,128)}, u32[]{:S(2)}) copy-start(f32[16,512]{1,0:T(8,128)} %diffusion.1) | copy-start | bytes 98308
  2.5 0.8 %copy-start.3 = (f32[16,512]{1,0:T(8,128)S(1)}, f32[16,512]{1,0:T(8,128)}, u32[]{:S(2)}) copy-start(f32[16,512]{1,0:T(8,128)} %velocity_x.1) | copy-start | bytes 98308
  3.2 0.8 %copy-start.4 = (f32[16,512]{1,0:T(8,128)S(1)}, f32[16,512]{1,0:T(8,128)}, u32[]{:S(2)}) copy-start(f32[16,512]{1,0:T(8,128)} %velocity_y.1) | copy-start | bytes 98308
  4.0 0.8 %copy-start.5 = (f32[16,512]{1,0:T(8,128)S(1)}, f32[16,512]{1,0:T(8,128)}, u32[]{:S(2)}) copy-start(f32[16,512]{1,0:T(8,128)} %source.1) | copy-start | bytes 98308

commit v3 on v2

v3 whole, which is shorter than its diff:
```python
import functools

import jax
import jax.numpy as jnp
from jax import lax
from jax.experimental import pallas as pl
from jax.experimental.pallas import tpu as pltpu
from jax.sharding import PartitionSpec as P

M = 8
NX = 4
NZ = 8
C = 4
R = 4
T = (8, 128)
W = 128 * C
NY = 8 * R
MESH = pl.DeviceIdType.MESH
BF16 = jnp.bfloat16
F32 = jnp.float32


def tile(ref, lead, r, c):
    return ref[(*lead, pl.ds(8 * r, 8), pl.ds(128 * c, 128))]


def load_state(ref, *lead, columns=C):
    return [[tile(ref, lead, r, c) for r in range(R)] for c in range(columns)]


def store_state(ref, v, *lead):
    for c, column in enumerate(v):
        for r in range(R):
            ref[(*lead, pl.ds(8 * r, 8), pl.ds(128 * c, 128))] = column[r]


def load_win(ref, *lead):
    return load_state(ref, *lead, columns=1)[0]


def store_win(ref, v, *lead):
    store_state(ref, [v], *lead)


def add(a, b):
    if isinstance(a, list):
        return [add(x, y) for x, y in zip(a, b)]
    return a + b


def sub(a, b):
    if isinstance(a, list):
        return [sub(x, y) for x, y in zip(a, b)]
    return a - b


def iota(shape, dim):
    return lax.broadcasted_iota(jnp.int32, shape, dim)


def at_row(column, r, di):
    carry, index = divmod(r + di, R)
    x = column[index]
    return x if carry == 0 else pltpu.roll(x, (-carry) % 8, 0)


def beside(v, width):
    ext = {c: v[c] for c in range(C)}
    for j in range(1, width + 1):
        ext[-j] = [pltpu.roll(x, 1, 1) for x in v[C - j]]
        ext[C - 1 + j] = [pltpu.roll(x, 127, 1) for x in v[j - 1]]
    return ext


def advance(states, coef, first, count, source=None):
    exts = [beside(v, count) for v in states]
    for j in range(count):
        width = count - 1 - j
        news = [{} for _ in exts]
        for c in range(-width, C + width):
            for n in news:
                n[c] = []
            for r in range(R):
                k0, kl, kr, ku, kd = (tile(coef, (k,), r, c - first) for k in range(5))
                plus = None if source is None else tile(source, (), r, c)
                for n, e in zip(news, exts):
                    new = (k0 * e[c][r] + kl * e[c - 1][r]) + (kr * e[c + 1][r] + ku * at_row(e[c], r, -1))
                    new = new + kd * at_row(e[c], r, 1)
                    n[c].append(new if plus is None else new + plus)
        exts = news
    return [[e[c] for c in range(C)] for e in exts]


def relax(states, coef, source):
    return lax.fori_loop(0, M, lambda _, s: advance(s, coef, 0, 1, source), states)


def move(v, coef, times, count=2, unroll=1):
    def some(_, s):
        for _ in range(unroll):
            s = advance(s, coef, -1, count)
        return s

    return lax.fori_loop(0, times, some, [v])[0]


ONE = [(0, 0), (0, -1), (0, 1), (-1, 0), (1, 0)]


def sums(a, b):
    out = []
    for d in a:
        for e in b:
            f = (d[0] + e[0], d[1] + e[1])
            if f not in out:
                out.append(f)
    return out


TWO = sums(ONE, ONE)
FOUR = sums(TWO, TWO)


def along(v, dj):
    return v if dj == 0 else [pltpu.roll(x, (-dj) % 128, 1) for x in v]


def win_apply(v, coef, offsets):
    moved = {dj: along(v, dj) for dj in sorted({d[1] for d in offsets})}
    out = []
    for r in range(R):
        parts = [None] * 4
        for n, (di, dj) in enumerate(offsets):
            term = tile(coef, (n,), r, 0) * at_row(moved[dj], r, di)
            parts[n % 4] = term if parts[n % 4] is None else parts[n % 4] + term
        out.append((parts[0] + parts[1]) + (parts[2] + parts[3]))
    return out


def compose(out, a, a_offsets, b, b_offsets, out_offsets):
    seen = set()
    for dj in sorted({d[1] for d in a_offsets}):
        for n, e in enumerate(b_offsets):
            moved = along(load_win(b, n), dj)
            for m, d in enumerate(a_offsets):
                if d[1] != dj:
                    continue
                k = out_offsets.index((d[0] + e[0], d[1] + e[1]))
                for r in range(R):
                    term = tile(a, (m,), r, 0) * at_row(moved, r, d[0])
                    if k in seen:
                        term = term + tile(out, (k,), r, 0)
                    out[k, pl.ds(8 * r, 8), :] = term
                seen.add(k)


def permuted(x, matrix):
    high = x.astype(BF16)
    rest = x - high.astype(F32)
    mid = rest.astype(BF16)
    low = (rest - mid.astype(F32)).astype(BF16)
    count = x.shape[0]
    parts = jnp.concatenate([high, mid, low], axis=0)
    out = jnp.dot(parts, matrix, preferred_element_type=F32)
    return (out[:count] + out[count : 2 * count]) + out[2 * count :]


def selector(row_of_column):
    return jnp.where(iota((W, W), 0) == row_of_column, 1.0, 0.0).astype(BF16)


def inner_place(column):
    return 128 * lax.rem(column, C) + lax.div(column, C)


def merged(own, other, band):
    lane = iota(T, 1)
    low = band == 0
    out = []
    for a, b in zip(own, other):
        w0, w1 = jnp.where(low, a, b), jnp.where(low, b, a)
        out.append(jnp.where(lane < 64, pltpu.roll(w0, 96, 1), pltpu.roll(w1, 32, 1)))
    return out


def kernel(
    n_tm, cpoints, initial, diffusion, velocity_x, velocity_y, source, out,
    raw, perm_in, perm_win, perm_out, c1, c8, c64, src, init, cw1, cw2, cw4, cwide, rows, cpi, rel, prl, relm, dfc,
    u_own, u_sib, u_sum, up, term, mid, lag, w1s, w1, u1, pz, t2own, t2sib, t2m, t2, rown, rsib, rm, rr, rri, t2i,
    fbuf, outi, outb, send, recv, loc,
):
    p = lax.axis_index("tm")
    s = lax.axis_index("space")
    x = lax.rem(p, NX)
    g = lax.div(p, NX)
    z = lax.rem(g, NZ)
    y = lax.div(g, NZ)
    n_y = n_tm // (NX * NZ)
    plane = NX * NZ
    other = 1 - s
    row0 = pl.multiple_of(16 * s, 16)
    band = pl.ds(row0, 16)
    base = 4 * s
    first_slab = p == 0

    def dev(tm, space):
        return {"tm": tm, "space": space}

    def cols(c):
        return pl.ds(pl.multiple_of(128 * c, 128), 128)

    barrier = pltpu.get_barrier_semaphore()

    def greet(tm, space):
        pl.semaphore_signal(barrier, inc=1, device_id=dev(tm, space), device_id_type=MESH)

    greet(p, other)
    for d in (4, 3, 5, 2, 6, 1, 7):
        greet(plane * y + NX * lax.rem(z + d, NZ) + x, s)
    for yy in range(n_y - 1):
        @pl.when(yy < y)
        def _():
            for xx in range(NX):
                greet(plane * yy + NX * z + xx, s)

    for d in (2, 1, 3):
        greet(NX * g + lax.rem(x + d, NX), s)
        greet(NX * g + lax.rem(x + d, NX), other)

    @pl.when(p > 0)
    def _():
        greet(p - 1, 0)
        greet(p - 1, 1)

    @pl.when(jnp.logical_and(x < 2, g > 0))
    def _():
        for xx in range(NX):
            greet(NX * (g - 1) + xx, s)

    fields = (diffusion, velocity_x, velocity_y, source, initial)
    for k, f in enumerate(fields):
        pltpu.make_async_copy(f, raw.at[k, band, :], loc.at[0]).start()
    pltpu.make_async_copy(cpoints.at[pl.ds(base, 4)], raw.at[pl.ds(5, 4), band, :], loc.at[0]).start()

    sends = 1 + 2 * (NX - 1) + (NZ - 1) + NX * (n_y - 1 - y)
    sends = sends + jnp.where(p < n_tm - 1, 2, 0) + jnp.where(g < n_tm // NX - 1, 2, 0)
    pl.semaphore_wait(barrier, sends)

    def remote(src_ref, dst_ref, to, send_idx, recv_idx):
        return pltpu.make_async_remote_copy(
            src_ref=src_ref, dst_ref=dst_ref, send_sem=send.at[send_idx], recv_sem=recv.at[recv_idx],
            device_id=to, device_id_type=MESH,
        )

    def whole(ref, idx):
        return remote(ref, ref, dev(p, other), idx, idx)

    for k, f in enumerate(fields):
        remote(f, raw.at[k, band, :], dev(p, other), 0, 0).start()
    remote(cpoints.at[pl.ds(4 * other, 4)], raw.at[pl.ds(5, 4), band, :], dev(p, other), 0, 0).start()
    sib = whole(raw.at[pl.ds(0, 9), band, :], 0)

    @pl.when(p < n_tm - 1)
    def _():
        for ss in range(2):
            remote(cpoints.at[pl.ds(6, 2)], raw.at[pl.ds(9, 2), band, :], dev(p + 1, ss), 1, 1).start()

    ahead = whole(raw.at[pl.ds(9, 2)], 1)

    line = iota((1, W), 1)
    perm_in[...] = selector(C * lax.rem(line, 128) + lax.div(line, 128))
    for ss in range(2):
        begin = 128 * lax.div(line, 128) + (64 * ss + W - 32)
        perm_win[:, pl.ds(W * ss, W)] = selector(inner_place(lax.rem(begin + lax.rem(line, 128), W)))

    pltpu.make_async_copy(raw.at[pl.ds(0, 9), band, :], raw.at[pl.ds(0, 9), band, :], loc.at[0]).wait()
    sib.wait_recv()

    def inward(first, count, emit):
        moved = permuted(raw[pl.ds(first, count)].reshape(count * NY, W), perm_in[...])
        for c in range(C):
            rows[c, pl.ds(0, count * NY), :] = moved[:, 128 * c : 128 * (c + 1)]
        for k in range(count):
            emit(k, [[rows[c, pl.ds(NY * k + r, 8, stride=R), :] for r in range(R)] for c in range(C)])

    got = {}

    def keep(k, v):
        if k < 3:
            got[k] = v
        elif k == 3:
            store_state(src, v)
        elif k == 4:
            store_state(init, v)
        else:
            store_state(cpi, v, k - 5)

    inward(0, 9, keep)

    sub_row = iota(T, 0)
    for c in range(C):
        for r in range(R):
            d, vx, vy = (got[k][c][r] for k in range(3))
            k0 = 4.0 * d + (jnp.abs(vx) + jnp.abs(vy))
            kl = d + jnp.maximum(vx, 0.0)
            kr = d - jnp.minimum(vx, 0.0)
            ku = d + jnp.maximum(vy, 0.0)
            kd = d - jnp.minimum(vy, 0.0)
            if r == 0:
                ku = jnp.where(sub_row == 0, 0.0, ku)
            if r == R - 1:
                kd = jnp.where(sub_row == 7, 0.0, kd)
            here = (pl.ds(8 * r, 8), pl.ds(128 * c, 128))
            wide = (pl.ds(8 * r, 8), pl.ds(128 * (c + 1), 128))
            for ref, scale, at in ((c1, 1.0, here), (c8, 8.0, wide), (c64, 64.0, wide)):
                ref[(0, *at)] = 1.0 - scale * k0
                for k, val in enumerate((kl, kr, ku, kd)):
                    ref[(k + 1, *at)] = scale * val

    for ref in (c8, c64):
        for k in range(5):
            for r in range(R):
                ref[k, pl.ds(8 * r, 8), pl.ds(0, 128)] = pltpu.roll(tile(ref, (k,), r, C), 1, 1)
                ref[k, pl.ds(8 * r, 8), pl.ds(128 * (C + 1), 128)] = pltpu.roll(tile(ref, (k,), r, 1), 127, 1)

    def relax_own(extra):
        once = relax([load_state(cpi, k) for k in range(4)] + extra, c1, src)
        for k in range(4):
            store_state(rel, once[k], base + 1 + k)
        twice = relax(once, c1, src)
        for k in range(4):
            store_state(prl, twice[k], base + 1 + k)
        if extra:
            store_state(mid, twice[4])

    opens = jnp.logical_and(first_slab, s == 0)

    @pl.when(opens)
    def _():
        relax_own([load_state(init)])

    @pl.when(jnp.logical_not(opens))
    def _():
        relax_own([])
        mid[...] = jnp.zeros_like(mid)

    head = sub(load_state(mid), load_state(rel, base + 1))

    def defect(k):
        return sub(load_state(prl, base + k - 1), load_state(rel, base + k))

    head, late = advance([head, defect(4)], c8, -1, 1)
    head = add(head, defect(2))
    late = add(late, load_state(prl, base + 4))
    (head,) = advance([head], c8, -1, 1)
    store_state(fbuf, add(head, defect(3)))
    store_state(term, late)

    @pl.when(s == 0)
    def _():
        v = move(load_state(fbuf), c8, 1)
        v = move(add(v, load_state(term)), c8, 5)
        store_state(u_own, v)
        store_state(term, advance([v], c64, -1, 1)[0])

    @pl.when(s == 1)
    def _():
        a, b = lax.fori_loop(
            0, 4, lambda _, v: advance(v, c8, -1, 2), [load_state(fbuf), load_state(term)]
        )
        store_state(u_own, a)
        b = move(b, c8, 3)
        store_state(term, add(advance([a], c64, -1, 1)[0], b))

    w1s[...] = permuted(term[...], perm_win[...])
    for d in (2, 1, 3, 0):
        for flip in (0, 1):
            if d == 0 and flip == 0:
                continue
            xx, ss = lax.rem(x + d, NX), lax.rem(s + flip, 2)
            remote(w1s.at[:, cols(NX * ss + xx)], w1.at[2 * x + s], dev(NX * g + xx, ss), 2, 2).start()
    to_x = whole(w1.at[pl.ds(0, 2 * NX - 1)], 2)
    own = cols(NX * s + x)
    store_win(w1, [w1s[pl.ds(8 * r, 8), own] for r in range(R)], 2 * x + s)

    half = pl.ds(base + 1, 4)
    remote(u_own, u_sib, dev(p, other), 3, 3).start()
    remote(rel.at[half], rel.at[half], dev(p, other), 3, 3).start()
    remote(prl.at[half], prl.at[half], dev(p, other), 3, 3).start()
    shared = whole(rel, 3)

    cwide[...] = permuted(
        c64[:, :, pl.ds(128, W)].reshape(5 * NY, W), perm_win[:, pl.ds(pl.multiple_of(W * s, W), W)]
    )
    for k in range(5):
        cw1[k] = cwide[pl.ds(NY * k, NY), cols(x)]
    compose(cw2, cw1, ONE, cw1, ONE, TWO)
    compose(cw4, cw2, TWO, cw2, TWO, FOUR)

    to_x.wait_recv()

    def group_term(i):
        return add(load_win(w1, 2 * i), load_win(w1, 2 * i + 1))

    a = add(win_apply(group_term(0), cw1, ONE), group_term(1))
    b = add(win_apply(group_term(2), cw1, ONE), group_term(3))
    store_win(u1, add(win_apply(a, cw2, TWO), b), z)

    for d in (4, 3, 5, 2, 6, 1, 7):
        zz = lax.rem(z + d, NZ)
        remote(u1.at[z], u1.at[z], dev(plane * y + NX * zz + x, s), 4, 16 + z).start()
    to_z = whole(u1.at[pl.ds(0, NZ - 1)], 4)

    perm_out[...] = selector(inner_place(line))
    shared.wait_recv()
    store_state(u_sum, add(load_state(u_own), load_state(u_sib)))
    to_up = remote(u_sum, up, dev(p + 1, s), 5, 5)

    @pl.when(p < n_tm - 1)
    def _():
        to_up.start()

    @pl.when(p > 0)
    def _():
        ahead.wait_recv()
        inward(9, 2, lambda k, v: store_state(cpi, v, k))

    @pl.when(first_slab)
    def _():
        up[...] = jnp.zeros_like(up)
        for k in range(2):
            store_state(cpi, load_state(init), k)

    v = relax([load_state(cpi, 0), load_state(cpi, 1)], c1, src)
    store_state(relm, v[0])
    store_state(rel, v[1], 0)

    @pl.when(first_slab)
    def _():
        store_state(relm, load_state(init))

    v = relax([load_state(relm), load_state(rel, 0)], c1, src)
    store_state(dfc, sub(v[0], load_state(rel, 0)), 0)
    store_state(prl, v[1], 0)

    def climb(k, v):
        d = sub(load_state(prl, k - 1), load_state(rel, k))
        store_state(dfc, d, k)
        return add(advance([v], c8, -1, 1)[0], d)

    v = lax.fori_loop(1, M, climb, load_state(dfc, 0))

    store_state(mid, v)

    pz[...] = jnp.zeros_like(pz)

    @pl.when(z != 0)
    def _():
        remote(u1.at[0], u1.at[0], dev(p, other), 4, 16).wait_recv()

    def ascend(zz, acc):
        @pl.when(z == zz)
        def _():
            store_win(pz, acc)

        @pl.when(z != zz)
        def _():
            remote(u1.at[zz], u1.at[zz], dev(p, other), 4, 16 + zz).wait_recv()

        return add(win_apply(acc, cw4, FOUR), load_win(u1, zz))

    store_win(t2own, lax.fori_loop(1, NZ, ascend, load_win(u1, 0)))
    swap_t = remote(t2own, t2sib, dev(p, other), 7, 7)
    swap_t.start()

    acc = load_win(pz)
    store_win(rown, acc, 0)
    for i in range(NX):
        acc = add(win_apply(acc, cw1, ONE), group_term(i))
        store_win(rown, acc, i + 1)
    swap_r = remote(rown, rsib, dev(p, other), 8, 8)
    swap_r.start()

    swap_t.wait_recv()
    store_win(t2m, merged(load_win(t2own), load_win(t2sib), s))
    for yy in range(1, n_y):
        @pl.when(yy > y)
        def _():
            for xx in range(NX):
                remote(
                    t2m, t2.at[y, :, cols(x)], dev(plane * yy + NX * z + xx, s), 8 + yy, 10 + y
                ).start()

    swap_r.wait_recv()
    for i in range(NX + 1):
        store_win(rm, merged(load_win(rown, i), load_win(rsib, i), s), i)
    to_r = []
    for i in range(NX):
        there = NX * g + 2 + i
        copy = remote(rm.at[pl.ds(i, 2)], rr.at[:, :, cols(x)], dev(there, s), 12 + i, 9)
        go = x != i + 2 if i < 2 else there < n_tm
        to_r.append((go, copy))

        @pl.when(go)
        def _():
            copy.start()

        if i < 2:
            @pl.when(x == i + 2)
            def _():
                for j in range(2):
                    rr[j, :, cols(x)] = rm[i + j]

    @pl.when(p > 0)
    def _():
        to_up.wait_recv()

    store_state(mid, add(load_state(mid), load_state(up)))
    to_lag = remote(mid, lag, dev(p + 1, s), 6, 6)

    @pl.when(p < n_tm - 1)
    def _():
        to_lag.start()

    @pl.when(p < 2)
    def _():
        rr[...] = jnp.zeros_like(rr)

    @pl.when(first_slab)
    def _():
        lag[...] = jnp.zeros_like(lag)

    @pl.when(x >= 2)
    def _():
        whole(rr.at[:, :, pl.ds(0, W - 128)], 9).wait_recv()

    @pl.when(jnp.logical_and(x < 2, g > 0))
    def _():
        whole(rr, 9).wait_recv()

    rri[...] = permuted(rr[...].reshape(2 * NY, W), perm_in[...]).reshape(2, NY, W)

    q = jnp.maximum(p - 2, 0)
    n = lax.rem(q, plane)
    yq = lax.div(q, plane)
    fbuf[...] = jnp.zeros_like(fbuf)
    for yy in range(n_y - 1):
        @pl.when(yy < y)
        def _():
            whole(t2.at[yy], 10 + yy).wait_recv()

    t2i[...] = permuted(t2[...].reshape((n_y - 1) * NY, W), perm_in[...]).reshape(n_y - 1, NY, W)
    for yy in range(n_y - 1):
        @pl.when(yy < yq)
        def _():
            f = load_state(t2i, yy)
            if yy > 0:
                f = add(move(load_state(fbuf), c64, plane // 8, 2, 4), f)
            store_state(fbuf, f)

    n = jnp.where(yq > 0, n, 0)
    f = move(load_state(fbuf), c64, lax.div(n, 2))
    f = move(f, c64, lax.rem(n, 2), 1)
    e = add(f, load_state(rri, 0))
    (f,) = advance([f], c64, -1, 1)
    last = add(add(f, load_state(rri, 1)), load_state(mid))

    def emit(k, value):
        for c in range(C):
            for r in range(R):
                rows[c, pl.ds(r, 8, stride=R), :] = value[c][r]
        for c in range(C):
            for t in range(2):
                outi[k, pl.ds(8 * t, 8), pl.ds(128 * c, 128)] = rows[c, pl.ds(pl.multiple_of(row0 + 8 * t, 8), 8), :]

    emit(M - 1, add(last, load_state(rel, M - 1)))

    def errors(k, v):
        v = add(advance([v], c8, -1, 1)[0], load_state(dfc, k))
        emit(k, add(v, load_state(rel, k)))
        return v

    @pl.when(p > 0)
    def _():
        to_lag.wait_recv()

    lax.fori_loop(0, M - 1, errors, add(load_state(lag), e))
    outb[...] = permuted(outi[...].reshape(M * 16, W), perm_out[...]).reshape(M, 16, W)
    done = pltpu.make_async_copy(outb, out, loc.at[1])
    done.start()

    sib.wait_send()

    @pl.when(p < n_tm - 1)
    def _():
        ahead.wait_send()
        to_up.wait_send()
        to_lag.wait_send()

    for copy in (to_x, shared, to_z, swap_t, swap_r):
        copy.wait_send()
    for yy in range(1, n_y):
        @pl.when(yy > y)
        def _():
            whole(t2.at[0], 8 + yy).wait_send()

    for go, copy in to_r:
        @pl.when(go)
        def _():
            copy.wait_send()

    done.wait()


def body(n_tm, *args):
    def vmem(*shape, dtype=F32):
        return pltpu.VMEM(shape, dtype)

    def state(*lead):
        return vmem(*lead, NY, W)

    def window(*lead):
        return vmem(*lead, NY, 128)

    square = vmem(W, W, dtype=BF16)
    scratch = [
        state(11), square, vmem(W, 2 * W, dtype=BF16), square,
        state(5), vmem(5, NY, W + 256), vmem(5, NY, W + 256), state(), state(),
        window(len(ONE)), window(len(TWO)), window(len(FOUR)), vmem(5 * NY, W),
        vmem(C, 9 * NY, 128), state(4), state(9), state(9), state(), state(M),
        state(), state(), state(), state(), state(), state(), state(),
        vmem(NY, 2 * W), window(2 * NX), window(NZ), window(),
        window(), window(), window(), state(n_tm // (NX * NZ) - 1),
        window(NX + 1), window(NX + 1), window(NX + 1), state(2), state(2), state(n_tm // (NX * NZ) - 1),
        state(), vmem(M, 16, W), vmem(M, 16, W),
        pltpu.SemaphoreType.DMA((16,)), pltpu.SemaphoreType.DMA((24,)), pltpu.SemaphoreType.DMA((2,)),
    ]
    return pl.pallas_call(
        functools.partial(kernel, n_tm),
        out_shape=jax.ShapeDtypeStruct(args[0].shape, F32),
        in_specs=[pl.BlockSpec(memory_space=pltpu.HBM)] * 6,
        out_specs=pl.BlockSpec(memory_space=pltpu.HBM),
        scratch_shapes=scratch,
        compiler_params=pltpu.CompilerParams(
            collective_id=0, has_side_effects=True, vmem_limit_bytes=60 * 1024 * 1024
        ),
    )(*args)


def solution(mesh):
    placed = (
        P("tm", "space", None),
        P("space", None),
        P("space", None),
        P("space", None),
        P("space", None),
        P("space", None),
    )
    return jax.shard_map(
        functools.partial(body, mesh.shape["tm"]),
        mesh=mesh, in_specs=placed, out_specs=P("tm", "space", None), check_vma=False,
    )
```

time: 48.6 us -> 41.6 us (0.86)
  local copies, waits for them, and re-layouts: 5.44 us -> 1.67 us
  Pallas kernels: 42.7 us -> 39.8 us
    unnamed x13 -> x1, local copies, waits for them, and re-layouts: 5.44 us -> 1.67 us
    pallas_call x1, Pallas kernels: 42.7 us -> 39.8 us  [body(): pl.pallas_call(functools.partial(kernel, n_tm), out_shape=jax.ShapeDtypeS...]
where the time goes in v3:
time: 41.6 us; the launch traced here: 41.5 us
  Pallas kernels  39.8 us (96%)
  local copies, waits for them, and re-layouts  1.67 us (4%)
    pallas_call x1, Pallas kernels, body(): pl.pallas_call(functools.partial(kernel, n_tm), out_shape=jax.ShapeDtypeS...  39.8 us
    unnamed x1, local copies, waits for them, and re-layouts  1.67 us

profile of v3, /device:TPU:25, one launch (start us, length us, event | category | flops | bytes accessed | tf_op | source)
XLA Modules:
  0.0 41.5 jit_solution(3460694309248510032)
XLA Ops:
  0.0 39.8 %shard_map.64 = f32[8,16,512]{2,1,0:T(8,128)} custom-call(f32[8,16,512]{2,1,0:T(8,128)} %cpoints.1, f32[16,512]{1,0:T(8,128)} %initial.1, f32[16,512]{1,0:T(8,128)} %diffusion.1, f32[16,512]{1,0:T(8,128)} %velocity_x.1, f32[16,512]{1,0:T(8,128)} %velocity_y.1, f32[16,512]{1,0:T(8,128)} %source.1), custom_call_target="tpu_custom_call" | custom-call | tf_op jit(solution)/shard_map/pallas_call | solution.py:638
  39.8 1.7 %copy.8 = f32[8,16,512]{2,1,0:T(8,128)} copy(f32[8,16,512]{2,1,0:T(8,128)} %shard_map.64) | data formatting | bytes 524288

commit v4 on v3

--- a/solution.py
+++ b/solution.py
@@ -187,7 +187,7 @@
     n_tm, cpoints, initial, diffusion, velocity_x, velocity_y, source, out,
     raw, perm_in, perm_win, perm_out, c1, c8, c64, src, init, cw1, cw2, cw4, cwide, rows, cpi, rel, prl, relm, dfc,
     u_own, u_sib, u_sum, up, term, mid, lag, w1s, w1, u1, pz, t2own, t2sib, t2m, t2, rown, rsib, rm, rr, rri, t2i,
-    fbuf, outi, outb, send, recv, loc,
+    fbuf, outi, outb, send, recv, loc, round_sem,
 ):
     p = lax.axis_index("tm")
     s = lax.axis_index("space")
@@ -209,42 +209,31 @@
     def cols(c):
         return pl.ds(pl.multiple_of(128 * c, 128), 128)
 
+    near = [dev(p, other)]
+    for d in (1, NX - 1):
+        near.append(dev(NX * g + lax.rem(x + d, NX), s))
+    for d in (1, NZ - 1):
+        near.append(dev(plane * y + NX * lax.rem(z + d, NZ) + x, s))
+    for d in (1, n_y - 1):
+        near.append(dev(plane * lax.rem(y + d, n_y) + NX * z + x, s))
+
+    def tell(sem):
+        for to in near:
+            pl.semaphore_signal(sem, inc=1, device_id=to, device_id_type=MESH)
+
+    def hear(sem):
+        pl.semaphore_wait(sem, len(near))
+
     barrier = pltpu.get_barrier_semaphore()
-
-    def greet(tm, space):
-        pl.semaphore_signal(barrier, inc=1, device_id=dev(tm, space), device_id_type=MESH)
-
-    greet(p, other)
-    for d in (4, 3, 5, 2, 6, 1, 7):
-        greet(plane * y + NX * lax.rem(z + d, NZ) + x, s)
-    for yy in range(n_y - 1):
-        @pl.when(yy < y)
-        def _():
-            for xx in range(NX):
-                greet(plane * yy + NX * z + xx, s)
-
-    for d in (2, 1, 3):
-        greet(NX * g + lax.rem(x + d, NX), s)
-        greet(NX * g + lax.rem(x + d, NX), other)
-
-    @pl.when(p > 0)
-    def _():
-        greet(p - 1, 0)
-        greet(p - 1, 1)
-
-    @pl.when(jnp.logical_and(x < 2, g > 0))
-    def _():
-        for xx in range(NX):
-            greet(NX * (g - 1) + xx, s)
+    tell(barrier)
 
     fields = (diffusion, velocity_x, velocity_y, source, initial)
     for k, f in enumerate(fields):
         pltpu.make_async_copy(f, raw.at[k, band, :], loc.at[0]).start()
     pltpu.make_async_copy(cpoints.at[pl.ds(base, 4)], raw.at[pl.ds(5, 4), band, :], loc.at[0]).start()
 
-    sends = 1 + 2 * (NX - 1) + (NZ - 1) + NX * (n_y - 1 - y)
-    sends = sends + jnp.where(p < n_tm - 1, 2, 0) + jnp.where(g < n_tm // NX - 1, 2, 0)
-    pl.semaphore_wait(barrier, sends)
+    hear(barrier)
+    tell(round_sem.at[0])
 
     def remote(src_ref, dst_ref, to, send_idx, recv_idx):
         return pltpu.make_async_remote_copy(
@@ -259,13 +248,6 @@
         remote(f, raw.at[k, band, :], dev(p, other), 0, 0).start()
     remote(cpoints.at[pl.ds(4 * other, 4)], raw.at[pl.ds(5, 4), band, :], dev(p, other), 0, 0).start()
     sib = whole(raw.at[pl.ds(0, 9), band, :], 0)
-
-    @pl.when(p < n_tm - 1)
-    def _():
-        for ss in range(2):
-            remote(cpoints.at[pl.ds(6, 2)], raw.at[pl.ds(9, 2), band, :], dev(p + 1, ss), 1, 1).start()
-
-    ahead = whole(raw.at[pl.ds(9, 2)], 1)
 
     line = iota((1, W), 1)
     perm_in[...] = selector(C * lax.rem(line, 128) + lax.div(line, 128))
@@ -296,6 +278,8 @@
             store_state(cpi, v, k - 5)
 
     inward(0, 9, keep)
+    hear(round_sem.at[0])
+    tell(round_sem.at[1])
 
     sub_row = iota(T, 0)
     for c in range(C):
@@ -344,6 +328,9 @@
         relax_own([])
         mid[...] = jnp.zeros_like(mid)
 
+    hear(round_sem.at[1])
+    tell(round_sem.at[2])
+
     head = sub(load_state(mid), load_state(rel, base + 1))
 
     def defect(k):
@@ -388,6 +375,15 @@
     remote(rel.at[half], rel.at[half], dev(p, other), 3, 3).start()
     remote(prl.at[half], prl.at[half], dev(p, other), 3, 3).start()
     shared = whole(rel, 3)
+
+    hear(round_sem.at[2])
+
+    @pl.when(p < n_tm - 1)
+    def _():
+        for ss in range(2):
+            remote(cpoints.at[pl.ds(6, 2)], raw.at[pl.ds(9, 2), band, :], dev(p + 1, ss), 1, 1).start()
+
+    ahead = whole(raw.at[pl.ds(9, 2)], 1)
 
     cwide[...] = permuted(
         c64[:, :, pl.ds(128, W)].reshape(5 * NY, W), perm_win[:, pl.ds(pl.multiple_of(W * s, W), W)]
@@ -634,6 +630,7 @@
         window(NX + 1), window(NX + 1), window(NX + 1), state(2), state(2), state(n_tm // (NX * NZ) - 1),
         state(), vmem(M, 16, W), vmem(M, 16, W),
         pltpu.SemaphoreType.DMA((16,)), pltpu.SemaphoreType.DMA((24,)), pltpu.SemaphoreType.DMA((2,)),
+        pltpu.SemaphoreType.REGULAR((3,)),
     ]
     return pl.pallas_call(
         functools.partial(kernel, n_tm),

time: 41.6 us -> 40.3 us (0.969)
  Pallas kernels: 39.8 us -> 38.5 us
    pallas_call x1, Pallas kernels: 39.8 us -> 38.5 us  [body(): pl.pallas_call(functools.partial(kernel, n_tm), out_shape=jax.ShapeDtypeS...]
where the time goes in v4:
time: 40.3 us; the launch traced here: 40.2 us
  Pallas kernels  38.5 us (96%)
  local copies, waits for them, and re-layouts  1.67 us (4%)
    pallas_call x1, Pallas kernels, body(): pl.pallas_call(functools.partial(kernel, n_tm), out_shape=jax.ShapeDtypeS...  38.5 us
    unnamed x1, local copies, waits for them, and re-layouts  1.67 us

profile of v4, /device:TPU:25, one launch (start us, length us, event | category | flops | bytes accessed | tf_op | source)
XLA Modules:
  0.0 40.2 jit_solution(1393501228054792648)
XLA Ops:
  0.0 38.5 %shard_map.64 = f32[8,16,512]{2,1,0:T(8,128)} custom-call(f32[8,16,512]{2,1,0:T(8,128)} %cpoints.1, f32[16,512]{1,0:T(8,128)} %initial.1, f32[16,512]{1,0:T(8,128)} %diffusion.1, f32[16,512]{1,0:T(8,128)} %velocity_x.1, f32[16,512]{1,0:T(8,128)} %velocity_y.1, f32[16,512]{1,0:T(8,128)} %source.1), custom_call_target="tpu_custom_call" | custom-call | tf_op jit(solution)/shard_map/pallas_call | solution.py:635
  38.5 1.7 %copy.8 = f32[8,16,512]{2,1,0:T(8,128)} copy(f32[8,16,512]{2,1,0:T(8,128)} %shard_map.64) | data formatting | bytes 524288

commit v5 on v4

--- a/solution.py
+++ b/solution.py
@@ -178,8 +178,7 @@
     low = band == 0
     out = []
     for a, b in zip(own, other):
-        w0, w1 = jnp.where(low, a, b), jnp.where(low, b, a)
-        out.append(jnp.where(lane < 64, pltpu.roll(w0, 96, 1), pltpu.roll(w1, 32, 1)))
+        out.append(jnp.where(low == (lane < 64), a, b))
     return out
 
 
@@ -253,7 +252,8 @@
     perm_in[...] = selector(C * lax.rem(line, 128) + lax.div(line, 128))
     for ss in range(2):
         begin = 128 * lax.div(line, 128) + (64 * ss + W - 32)
-        perm_win[:, pl.ds(W * ss, W)] = selector(inner_place(lax.rem(begin + lax.rem(line, 128), W)))
+        turned = lax.rem(lax.rem(line, 128) + 32 + 64 * ss, 128)
+        perm_win[:, pl.ds(W * ss, W)] = selector(inner_place(lax.rem(begin + turned, W)))
 
     pltpu.make_async_copy(raw.at[pl.ds(0, 9), band, :], raw.at[pl.ds(0, 9), band, :], loc.at[0]).wait()
     sib.wait_recv()
@@ -479,7 +479,7 @@
 
     swap_t.wait_recv()
     store_win(t2m, merged(load_win(t2own), load_win(t2sib), s))
-    for yy in range(1, n_y):
+    for yy in range(n_y - 1, 0, -1):
         @pl.when(yy > y)
         def _():
             for xx in range(NX):
@@ -526,37 +526,41 @@
     def _():
         lag[...] = jnp.zeros_like(lag)
 
-    @pl.when(x >= 2)
-    def _():
-        whole(rr.at[:, :, pl.ds(0, W - 128)], 9).wait_recv()
-
-    @pl.when(jnp.logical_and(x < 2, g > 0))
-    def _():
-        whole(rr, 9).wait_recv()
-
-    rri[...] = permuted(rr[...].reshape(2 * NY, W), perm_in[...]).reshape(2, NY, W)
-
     q = jnp.maximum(p - 2, 0)
     n = lax.rem(q, plane)
     yq = lax.div(q, plane)
     fbuf[...] = jnp.zeros_like(fbuf)
     for yy in range(n_y - 1):
-        @pl.when(yy < y)
-        def _():
+        @pl.when(yy < yq)
+        def _():
+            if yy > 0:
+                v = move(load_state(fbuf), c64, (plane - 4) // 4, 2, 2)
             whole(t2.at[yy], 10 + yy).wait_recv()
-
-    t2i[...] = permuted(t2[...].reshape((n_y - 1) * NY, W), perm_in[...]).reshape(n_y - 1, NY, W)
-    for yy in range(n_y - 1):
-        @pl.when(yy < yq)
-        def _():
-            f = load_state(t2i, yy)
+            t2i[...] = permuted(t2[yy], perm_in[...])
             if yy > 0:
-                f = add(move(load_state(fbuf), c64, plane // 8, 2, 4), f)
-            store_state(fbuf, f)
+                for _ in range(2):
+                    (v,) = advance([v], c64, -1, 2)
+            f = load_state(t2i)
+            store_state(fbuf, add(v, f) if yy > 0 else f)
 
     n = jnp.where(yq > 0, n, 0)
     f = move(load_state(fbuf), c64, lax.div(n, 2))
     f = move(f, c64, lax.rem(n, 2), 1)
+
+    @pl.when(x >= 2)
+    def _():
+        whole(rr.at[:, :, pl.ds(0, W - 128)], 9).wait_recv()
+
+    @pl.when(jnp.logical_and(x < 2, g > 0))
+    def _():
+        whole(rr, 9).wait_recv()
+
+    @pl.when(p > 0)
+    def _():
+        to_lag.wait_recv()
+
+    rri[...] = permuted(rr[...].reshape(2 * NY, W), perm_in[...]).reshape(2, NY, W)
+
     e = add(f, load_state(rri, 0))
     (f,) = advance([f], c64, -1, 1)
     last = add(add(f, load_state(rri, 1)), load_state(mid))
@@ -576,14 +580,15 @@
         emit(k, add(v, load_state(rel, k)))
         return v
 
-    @pl.when(p > 0)
-    def _():
-        to_lag.wait_recv()
-
     lax.fori_loop(0, M - 1, errors, add(load_state(lag), e))
     outb[...] = permuted(outi[...].reshape(M * 16, W), perm_out[...]).reshape(M, 16, W)
     done = pltpu.make_async_copy(outb, out, loc.at[1])
     done.start()
+
+    for yy in range(n_y - 1):
+        @pl.when(jnp.logical_and(yy >= yq, yy < y))
+        def _():
+            whole(t2.at[yy], 10 + yy).wait_recv()
 
     sib.wait_send()
 
@@ -627,7 +632,7 @@
         state(), state(), state(), state(), state(), state(), state(),
         vmem(NY, 2 * W), window(2 * NX), window(NZ), window(),
         window(), window(), window(), state(n_tm // (NX * NZ) - 1),
-        window(NX + 1), window(NX + 1), window(NX + 1), state(2), state(2), state(n_tm // (NX * NZ) - 1),
+        window(NX + 1), window(NX + 1), window(NX + 1), state(2), state(2), state(),
         state(), vmem(M, 16, W), vmem(M, 16, W),
         pltpu.SemaphoreType.DMA((16,)), pltpu.SemaphoreType.DMA((24,)), pltpu.SemaphoreType.DMA((2,)),
         pltpu.SemaphoreType.REGULAR((3,)),

time: 40.3 us -> 39.8 us (0.988)
  the two profiles are of different devices: /device:TPU:25 before, /device:TPU:17 now
where the time goes in v5:
time: 39.8 us; the launch traced here: 39.7 us
  Pallas kernels  38.1 us (96%)
  local copies, waits for them, and re-layouts  1.67 us (4%)
    pallas_call x1, Pallas kernels, body(): pl.pallas_call(functools.partial(kernel, n_tm), out_shape=jax.ShapeDtypeS...  38.1 us
    unnamed x1, local copies, waits for them, and re-layouts  1.67 us

profile of v5, /device:TPU:17, one launch (start us, length us, event | category | flops | bytes accessed | tf_op | source)
XLA Modules:
  0.0 39.7 jit_solution(16638988770062361536)
XLA Ops:
  0.0 38.1 %shard_map.64 = f32[8,16,512]{2,1,0:T(8,128)} custom-call(f32[8,16,512]{2,1,0:T(8,128)} %cpoints.1, f32[16,512]{1,0:T(8,128)} %initial.1, f32[16,512]{1,0:T(8,128)} %diffusion.1, f32[16,512]{1,0:T(8,128)} %velocity_x.1, f32[16,512]{1,0:T(8,128)} %velocity_y.1, f32[16,512]{1,0:T(8,128)} %source.1), custom_call_target="tpu_custom_call" | custom-call | tf_op jit(solution)/shard_map/pallas_call | solution.py:640
  38.1 1.7 %copy.8 = f32[8,16,512]{2,1,0:T(8,128)} copy(f32[8,16,512]{2,1,0:T(8,128)} %shard_map.64) | data formatting | bytes 524288

commit v6 on v5

--- a/solution.py
+++ b/solution.py
@@ -89,6 +89,18 @@
                     n[c].append(new if plus is None else new + plus)
         exts = news
     return [[e[c] for c in range(C)] for e in exts]
+
+
+def two_steps(v, before, after, coef):
+    def cell(e, r, c):
+        k0, kl, kr, ku, kd = (tile(coef, (k,), r, c + 1) for k in range(5))
+        new = (k0 * e[c][r] + kl * e[c - 1][r]) + (kr * e[c + 1][r] + ku * at_row(e[c], r, -1))
+        return new + kd * at_row(e[c], r, 1)
+
+    ext, plus = beside(v, 2), beside(before, 1)
+    one = {c: [cell(ext, r, c) + plus[c][r] for r in range(R)] for c in range(-1, C + 1)}
+    two = [[cell(one, r, c) + after[c][r] for r in range(R)] for c in range(C)]
+    return [one[c] for c in range(C)], two
 
 
 def relax(states, coef, source):
@@ -255,13 +267,20 @@
         turned = lax.rem(lax.rem(line, 128) + 32 + 64 * ss, 128)
         perm_win[:, pl.ds(W * ss, W)] = selector(inner_place(lax.rem(begin + turned, W)))
 
+    def columns_moved(first, count, at):
+        moved = permuted(raw[pl.ds(first, count), pl.ds(at, 16), :].reshape(count * 16, W), perm_in[...])
+        for k in range(count):
+            for c in range(C):
+                rows[c, pl.ds(pl.multiple_of(NY * k + at, 16), 16), :] = (
+                    moved[16 * k : 16 * (k + 1), 128 * c : 128 * (c + 1)]
+                )
+
     pltpu.make_async_copy(raw.at[pl.ds(0, 9), band, :], raw.at[pl.ds(0, 9), band, :], loc.at[0]).wait()
+    columns_moved(0, 9, row0)
     sib.wait_recv()
-
-    def inward(first, count, emit):
-        moved = permuted(raw[pl.ds(first, count)].reshape(count * NY, W), perm_in[...])
-        for c in range(C):
-            rows[c, pl.ds(0, count * NY), :] = moved[:, 128 * c : 128 * (c + 1)]
+    columns_moved(0, 9, pl.multiple_of(16 * other, 16))
+
+    def inward(count, emit):
         for k in range(count):
             emit(k, [[rows[c, pl.ds(NY * k + r, 8, stride=R), :] for r in range(R)] for c in range(C)])
 
@@ -277,7 +296,7 @@
         else:
             store_state(cpi, v, k - 5)
 
-    inward(0, 9, keep)
+    inward(9, keep)
     hear(round_sem.at[0])
     tell(round_sem.at[1])
 
@@ -419,7 +438,9 @@
     @pl.when(p > 0)
     def _():
         ahead.wait_recv()
-        inward(9, 2, lambda k, v: store_state(cpi, v, k))
+        for ss in range(2):
+            columns_moved(9, 2, 16 * ss)
+        inward(2, lambda k, v: store_state(cpi, v, k))
 
     @pl.when(first_slab)
     def _():
@@ -479,7 +500,7 @@
 
     swap_t.wait_recv()
     store_win(t2m, merged(load_win(t2own), load_win(t2sib), s))
-    for yy in range(n_y - 1, 0, -1):
+    for yy in (2, 3, 1):
         @pl.when(yy > y)
         def _():
             for xx in range(NX):
@@ -575,12 +596,16 @@
 
     emit(M - 1, add(last, load_state(rel, M - 1)))
 
-    def errors(k, v):
-        v = add(advance([v], c8, -1, 1)[0], load_state(dfc, k))
-        emit(k, add(v, load_state(rel, k)))
-        return v
-
-    lax.fori_loop(0, M - 1, errors, add(load_state(lag), e))
+    def errors(i, v):
+        k = 2 * i
+        one, two = two_steps(v, load_state(dfc, k), load_state(dfc, k + 1), c8)
+        emit(k, add(one, load_state(rel, k)))
+        emit(k + 1, add(two, load_state(rel, k + 1)))
+        return two
+
+    v = lax.fori_loop(0, M // 2 - 1, errors, add(load_state(lag), e))
+    v = add(advance([v], c8, -1, 1)[0], load_state(dfc, M - 2))
+    emit(M - 2, add(v, load_state(rel, M - 2)))
     outb[...] = permuted(outi[...].reshape(M * 16, W), perm_out[...]).reshape(M, 16, W)
     done = pltpu.make_async_copy(outb, out, loc.at[1])
     done.start()

time: 39.8 us -> 39.3 us (0.987)
  the two profiles are of different devices: /device:TPU:17 before, /device:TPU:25 now
where the time goes in v6:
time: 39.3 us; the launch traced here: 39.2 us
  Pallas kernels  37.5 us (95%)
  local copies, waits for them, and re-layouts  1.67 us (4%)
    pallas_call x1, Pallas kernels, body(): pl.pallas_call(functools.partial(kernel, n_tm), out_shape=jax.ShapeDtypeS...  37.5 us
    unnamed x1, local copies, waits for them, and re-layouts  1.67 us

profile of v6, /device:TPU:25, one launch (start us, length us, event | category | flops | bytes accessed | tf_op | source)
XLA Modules:
  0.0 39.2 jit_solution(2061354030977205503)
XLA Ops:
  0.0 37.5 %shard_map.64 = f32[8,16,512]{2,1,0:T(8,128)} custom-call(f32[8,16,512]{2,1,0:T(8,128)} %cpoints.1, f32[16,512]{1,0:T(8,128)} %initial.1, f32[16,512]{1,0:T(8,128)} %diffusion.1, f32[16,512]{1,0:T(8,128)} %velocity_x.1, f32[16,512]{1,0:T(8,128)} %velocity_y.1, f32[16,512]{1,0:T(8,128)} %source.1), custom_call_target="tpu_custom_call" | custom-call | tf_op jit(solution)/shard_map/pallas_call | solution.py:665
  37.5 1.7 %copy.8 = f32[8,16,512]{2,1,0:T(8,128)} copy(f32[8,16,512]{2,1,0:T(8,128)} %shard_map.64) | data formatting | bytes 524288

commit v7 on v6

--- a/solution.py
+++ b/solution.py
@@ -435,40 +435,6 @@
     def _():
         to_up.start()
 
-    @pl.when(p > 0)
-    def _():
-        ahead.wait_recv()
-        for ss in range(2):
-            columns_moved(9, 2, 16 * ss)
-        inward(2, lambda k, v: store_state(cpi, v, k))
-
-    @pl.when(first_slab)
-    def _():
-        up[...] = jnp.zeros_like(up)
-        for k in range(2):
-            store_state(cpi, load_state(init), k)
-
-    v = relax([load_state(cpi, 0), load_state(cpi, 1)], c1, src)
-    store_state(relm, v[0])
-    store_state(rel, v[1], 0)
-
-    @pl.when(first_slab)
-    def _():
-        store_state(relm, load_state(init))
-
-    v = relax([load_state(relm), load_state(rel, 0)], c1, src)
-    store_state(dfc, sub(v[0], load_state(rel, 0)), 0)
-    store_state(prl, v[1], 0)
-
-    def climb(k, v):
-        d = sub(load_state(prl, k - 1), load_state(rel, k))
-        store_state(dfc, d, k)
-        return add(advance([v], c8, -1, 1)[0], d)
-
-    v = lax.fori_loop(1, M, climb, load_state(dfc, 0))
-
-    store_state(mid, v)
-
     pz[...] = jnp.zeros_like(pz)
 
     @pl.when(z != 0)
@@ -527,6 +493,40 @@
             def _():
                 for j in range(2):
                     rr[j, :, cols(x)] = rm[i + j]
+
+    @pl.when(p > 0)
+    def _():
+        ahead.wait_recv()
+        for ss in range(2):
+            columns_moved(9, 2, 16 * ss)
+        inward(2, lambda k, v: store_state(cpi, v, k))
+
+    @pl.when(first_slab)
+    def _():
+        up[...] = jnp.zeros_like(up)
+        for k in range(2):
+            store_state(cpi, load_state(init), k)
+
+    v = relax([load_state(cpi, 0), load_state(cpi, 1)], c1, src)
+    store_state(relm, v[0])
+    store_state(rel, v[1], 0)
+
+    @pl.when(first_slab)
+    def _():
+        store_state(relm, load_state(init))
+
+    v = relax([load_state(relm), load_state(rel, 0)], c1, src)
+    store_state(dfc, sub(v[0], load_state(rel, 0)), 0)
+    store_state(prl, v[1], 0)
+
+    def climb(k, v):
+        d = sub(load_state(prl, k - 1), load_state(rel, k))
+        store_state(dfc, d, k)
+        return add(advance([v], c8, -1, 1)[0], d)
+
+    v = lax.fori_loop(1, M, climb, load_state(dfc, 0))
+
+    store_state(mid, v)
 
     @pl.when(p > 0)
     def _():

time: 39.3 us -> 39.1 us (level)
  the two profiles are of different devices: /device:TPU:25 before, /device:TPU:17 now
where the time goes in v7:
time: 39.1 us; the launch traced here: 39 us
  Pallas kernels  37.3 us (95%)
  local copies, waits for them, and re-layouts  1.67 us (4%)
    pallas_call x1, Pallas kernels, body(): pl.pallas_call(functools.partial(kernel, n_tm), out_shape=jax.ShapeDtypeS...  37.3 us
    unnamed x1, local copies, waits for them, and re-layouts  1.67 us

profile of v7, /device:TPU:17, one launch (start us, length us, event | category | flops | bytes accessed | tf_op | source)
XLA Modules:
  0.0 39.0 jit_solution(12134075634449393623)
XLA Ops:
  0.0 37.3 %shard_map.64 = f32[8,16,512]{2,1,0:T(8,128)} custom-call(f32[8,16,512]{2,1,0:T(8,128)} %cpoints.1, f32[16,512]{1,0:T(8,128)} %initial.1, f32[16,512]{1,0:T(8,128)} %diffusion.1, f32[16,512]{1,0:T(8,128)} %velocity_x.1, f32[16,512]{1,0:T(8,128)} %velocity_y.1, f32[16,512]{1,0:T(8,128)} %source.1), custom_call_target="tpu_custom_call" | custom-call | tf_op jit(solution)/shard_map/pallas_call | solution.py:665
  37.3 1.7 %copy.8 = f32[8,16,512]{2,1,0:T(8,128)} copy(f32[8,16,512]{2,1,0:T(8,128)} %shard_map.64) | data formatting | bytes 524288

commit v8 on v7

--- a/solution.py
+++ b/solution.py
@@ -565,7 +565,8 @@
             store_state(fbuf, add(v, f) if yy > 0 else f)
 
     n = jnp.where(yq > 0, n, 0)
-    f = move(load_state(fbuf), c64, lax.div(n, 2))
+    f = move(load_state(fbuf), c64, lax.div(n, 4), 2, 2)
+    f = move(f, c64, lax.div(lax.rem(n, 4), 2))
     f = move(f, c64, lax.rem(n, 2), 1)
 
     @pl.when(x >= 2)

time: 39.1 us -> 39 us (level)
  no operation moved by 1% of the time
where the time goes in v8:
time: 39 us; the launch traced here: 38.9 us
  Pallas kernels  37.3 us (96%)
  local copies, waits for them, and re-layouts  1.67 us (4%)
    pallas_call x1, Pallas kernels, body(): pl.pallas_call(functools.partial(kernel, n_tm), out_shape=jax.ShapeDtypeS...  37.3 us
    unnamed x1, local copies, waits for them, and re-layouts  1.67 us

profile of v8, /device:TPU:17, one launch (start us, length us, event | category | flops | bytes accessed | tf_op | source)
XLA Modules:
  0.0 38.9 jit_solution(16592506281553795921)
XLA Ops:
  0.0 37.3 %shard_map.64 = f32[8,16,512]{2,1,0:T(8,128)} custom-call(f32[8,16,512]{2,1,0:T(8,128)} %cpoints.1, f32[16,512]{1,0:T(8,128)} %initial.1, f32[16,512]{1,0:T(8,128)} %diffusion.1, f32[16,512]{1,0:T(8,128)} %velocity_x.1, f32[16,512]{1,0:T(8,128)} %velocity_y.1, f32[16,512]{1,0:T(8,128)} %source.1), custom_call_target="tpu_custom_call" | custom-call | tf_op jit(solution)/shard_map/pallas_call | solution.py:666
  37.3 1.7 %copy.8 = f32[8,16,512]{2,1,0:T(8,128)} copy(f32[8,16,512]{2,1,0:T(8,128)} %shard_map.64) | data formatting | bytes 524288
